TPU v7x, 32 devices: a whole 2x2x4 slice. The times are simulated.
32 devices in a mesh: groups: 2 (over x), seq: 16 (over z, y, core).
Axes of the slice: x: 2, y: 2, z: 4, core: 2. Of those that a mesh axis runs over, the one named last changes fastest.
Arguments:
- queries: bfloat16 [96, 8192], P(('groups', 'seq')), parts along dimension 0, may hold values from -9 to 9, as said below
- key_rows: bfloat16 [8192, 8192], P(('groups', 'seq')), parts along dimension 0, may hold values from -9 to 9, as said below
- value_rows: bfloat16 [8192, 8192], P(('groups', 'seq')), parts along dimension 0, may hold values from -6 to 6
- out_weight: bfloat16 [8192, 4096], P('seq'), may hold values from -6 to 6
- levels: int32 [3, 96], P(None, ('groups', 'seq')), parts along dimension 1, may hold values from 0 to 8
- owner_map: int32 [3, 96], P(None, ('groups', 'seq')), parts along dimension 1, may hold values from 0 to 47, each once within a row
Outputs:
- base_update: bfloat16 [96, 4096], P(('groups', 'seq')), parts along dimension 0
There are 2 independent parts, one for each index of `groups`. A program takes and returns all parts, laid end to end along the dimension named above; an argument that names none is the same for every part. Nothing has to cross between parts.
Inputs may be any that keep to these rules, and one draw needn't show every extreme that they name: queries: of order one, a few entries larger. key_rows: of order one, a few entries larger. Each row of owner_map names every base query token once; it stands in for a resampling onto base positions.
All inputs are finite; a program needn't handle non-finite values.
Results may differ from a plain program's by a relative error of at most 0.02.
Values may be sent and summed in bfloat16 or wider, within the bound.
A program may use at most 128 MiB of HBM per device.

v0:
```python
import jax
import jax.numpy as jnp
from jax import lax
from jax.sharding import PartitionSpec as P

HD = 128
HEADS = 16
CONTROLS = 3
LEVELS = 8


def local_block(operands):
    query_block, key_block, value_block = operands
    scores = jnp.einsum(
        "qph,kph->pqk", query_block, key_block, preferred_element_type=jnp.float32
    ) * HD ** (-0.5)
    peak = jnp.max(scores, axis=2)
    expo = jnp.exp(scores - peak[:, :, None])
    total = jnp.sum(expo, axis=2)
    weighted = jnp.einsum(
        "pqk,kph->pqh", expo.astype(jnp.bfloat16), value_block, preferred_element_type=jnp.float32
    )
    return (weighted, peak, total)


def on_device(queries, key_rows, value_rows, out_weight, levels, owner_map):
    seq_count = lax.axis_size("seq")
    query_dev = queries.shape[0]
    total_queries = query_dev * seq_count
    pairs = queries.shape[1] // HD
    heads_dev = out_weight.shape[0] // HD
    level_all, owner_all = (
        lax.all_gather(levels, "seq", axis=1, tiled=True),
        lax.all_gather(owner_map, "seq", axis=1, tiled=True),
    )
    gathered = lax.all_gather(queries, "seq", axis=0, tiled=True)
    blocks = pairs // 8
    query_split = gathered.reshape(total_queries, blocks, 8, HD).transpose(1, 0, 2, 3)
    key_split = key_rows.reshape(-1, blocks, 8, HD).transpose(1, 0, 2, 3)
    value_split = value_rows.reshape(-1, blocks, 8, HD).transpose(1, 0, 2, 3)
    weighted, peak, total = lax.map(local_block, (query_split, key_split, value_split))
    weighted = weighted.reshape(pairs, total_queries, HD)
    peak = peak.reshape(pairs, total_queries)
    total = total.reshape(pairs, total_queries)
    part_out, part_peak, part_total = (
        lax.all_to_all(
            weighted[:, None].astype(jnp.bfloat16), "seq", split_axis=0, concat_axis=1, tiled=True
        ).astype(jnp.float32),
        lax.all_to_all(
            peak[:, None].astype(jnp.bfloat16), "seq", split_axis=0, concat_axis=1, tiled=True
        ).astype(jnp.float32),
        lax.all_to_all(
            total[:, None].astype(jnp.bfloat16), "seq", split_axis=0, concat_axis=1, tiled=True
        ).astype(jnp.float32),
    )
    best = jnp.max(part_peak, axis=1)
    factor = jnp.exp(part_peak - best[:, None])
    numer = jnp.sum(factor[..., None] * part_out, axis=1)
    denom = jnp.sum(factor * part_total, axis=1)
    attended = (numer / denom[..., None]).astype(jnp.bfloat16)
    section = lax.axis_index("seq") * heads_dev // HEADS
    is_base = section >= CONTROLS
    control = jnp.minimum(section, CONTROLS - 1)
    owner_here = lax.dynamic_index_in_dim(owner_all, control, 0, keepdims=False)
    level_here = lax.dynamic_index_in_dim(level_all, control, 0, keepdims=False)
    positions = jnp.arange(total_queries, dtype=jnp.int32)
    owner_here = jnp.where(is_base, positions, owner_here)
    level_here = jnp.where(is_base, LEVELS, level_here)
    selector = owner_here[None, :] == positions[:, None]
    chosen = jnp.einsum(
        "bt,pth->bph", selector.astype(jnp.bfloat16), attended, preferred_element_type=jnp.float32
    ).astype(jnp.bfloat16)
    mixed = chosen.reshape(total_queries, heads_dev * HD)
    row_weight = jnp.dot(selector.astype(jnp.float32), level_here.astype(jnp.float32)) / LEVELS
    summed = lax.psum_scatter(
        jnp.dot(mixed, out_weight, preferred_element_type=jnp.float32) * row_weight[:, None],
        "seq",
        scatter_dimension=0,
        tiled=True,
    )
    return summed.astype(jnp.bfloat16)


def solution(mesh):
    return jax.shard_map(
        on_device,
        mesh=mesh,
        in_specs=(
            P(("groups", "seq"), None),
            P(("groups", "seq"), None),
            P(("groups", "seq"), None),
            P("seq", None),
            P(None, ("groups", "seq")),
            P(None, ("groups", "seq")),
        ),
        out_specs=P(("groups", "seq"), None),
        check_vma=False,
    )
```

profile of v0, /device:TPU:0, one launch (start us, length us, event | category | flops | bytes accessed | tf_op | source)
XLA Modules:
  0.0 215.2 jit_solution(13509341424326010347)
XLA Ops:
  0.0 26.3 %all-gather.1 = bf16[16,3,8192]{2,1,0:T(4,128)(2,1)S(1)} all-gather(bf16[1,3,8192]{2,1,0:T(4,128)(2,1)} %bitcast.100), channel_id=1, replica_groups=mesh['groups'=2,'seq'=16] {'seq'}, dimensions={0}, use_global_device_ids=true | all-gather | bytes 835584 | tf_op jit(solution)/shard_map/all_gather | solution.py:36
  26.3 1.1 reshape.79
  27.4 6.4 %copy.33 = bf16[256,8192]{0,1:T(8,128)(2,1)} copy(bf16[256,8192]{1,0:T(8,128)(2,1)} %param.9) | data formatting | bytes 8388608 | tf_op args[1]
  33.8 6.4 %copy.34 = bf16[256,8192]{0,1:T(8,128)(2,1)} copy(bf16[256,8192]{1,0:T(8,128)(2,1)} %param.10) | data formatting | bytes 8388608 | tf_op args[2]
  40.2 0.0 copy-start
  40.2 0.0 copy-start.1
  40.2 0.0 copy-start.2
  40.2 29.4 %while.14 = (s32[]{:T(128)}, bf16[8,8,48,128]{3,2,1,0:T(8,128)(2,1)}, bf16[8,8,48]{2,1,0:T(8,128)(2,1)S(1)}, bf16[8,8,48]{2,1,0:T(8,128)(2,1)S(1)}, bf16[8,48,8,...) while((s32[]{:T(128)}, ...), condition=%wide.region_3.4_spmd, body=%wide.region_0.3_spmd.sunk | while | flops 50920704 | bytes 2738541 | solution.py:41
  40.3 1.3 fusion.35
  41.6 2.0 fusion.36
  43.7 0.2 fusion.37
  43.9 1.3 fusion.35
  45.3 2.0 fusion.36
  47.3 0.2 fusion.37
  47.6 1.3 fusion.35
  49.0 2.0 fusion.36
  51.0 0.2 fusion.37
  51.3 1.3 fusion.35
  52.6 2.0 fusion.36
  54.7 0.2 fusion.37
  55.0 1.3 fusion.35
  56.3 2.0 fusion.36
  58.3 0.2 fusion.37
  58.6 1.3 fusion.35
  60.0 2.0 fusion.36
  62.0 0.2 fusion.37
  62.3 1.3 fusion.35
  63.7 2.0 fusion.36
  65.7 0.2 fusion.37
  66.0 1.3 fusion.35
  67.3 2.0 fusion.36
  69.4 0.2 fusion.37
  69.6 0.6 copy.39
  70.3 3.5 %all-to-all-start.2 = ((bf16[64,1,48]{2,1,0:T(2,128)(2,1)}), bf16[64,1,48]{2,1,0:T(2,128)(2,1)S(1)}, u32[]{:S(2)}, u32[]{:S(2)}) async-start(bf16[64,1,48]{2,1,0:T(2,128)(2,1)} %copy.39), calls=%async_computation.2 | async-start | bytes 65536 | tf_op jit(solution)/shard_map/all_to_all | solution.py:52
  73.8 6.6 %all-to-all-done.2 = bf16[64,1,48]{2,1,0:T(2,128)(2,1)S(1)} async-done(((bf16[64,1,48]{2,1,0:T(2,128)(2,1)}), bf16[64,1,48]{2,1,0:T(2,128)(2,1)S(1)}, u32[]{:S(2)}, u32[]{:S(2)}) %all-to-all-start.2) | async-done | bytes 6176 | tf_op jit(solution)/shard_map/all_to_all | solution.py:52
  80.4 9.2 %all_to_all.33 = bf16[64,1,48]{2,1,0:T(2,128)(2,1)S(1)} all-to-all(bf16[64,1,48]{2,1,0:T(2,128)(2,1)S(1)} %copy.38), channel_id=1, replica_groups=mesh['groups'=2,'seq'=16] {'seq'}, dimensions={0} | all-to-all | bytes 12288 | tf_op jit(solution)/shard_map/all_to_all | solution.py:49
  89.6 3.6 %all-to-all-start.1 = ((bf16[64,1,48,128]{3,2,1,0:T(8,128)(2,1)}), bf16[64,1,48,128]{3,2,1,0:T(8,128)(2,1)S(1)}, u32[]{:S(2)}, u32[]{:S(2)}) async-start(bf16[64,1,48,128]{3,2,1,0:T(8,128)(2,1)} %bitcast.20), calls=%async_computation.1 | async-start | bytes 1572864 | tf_op jit(solution)/shard_map/all_to_all | solution.py:46
  93.2 0.0 copy-done
  93.2 0.1 copy.41
  93.3 29.1 %all-gather.2 = s32[16,3,3]{2,1,0:T(4,128)S(1)} all-gather(s32[1,3,3]{2,1,0:T(4,128)S(1)} %bitcast.103), channel_id=1, replica_groups=mesh['groups'=2,'seq'=16] {'seq'}, dimensions={0}, use_global_device_ids=true | all-gather | bytes 612 | tf_op jit(solution)/shard_map/all_gather | solution.py:33
  122.4 0.0 copy-done.1
  122.4 0.1 copy.31
  122.5 20.2 %all-gather = s32[16,3,3]{2,1,0:T(4,128)S(1)} all-gather(s32[1,3,3]{2,1,0:T(4,128)S(1)} %bitcast.104), channel_id=1, replica_groups=mesh['groups'=2,'seq'=16] {'seq'}, dimensions={0}, use_global_device_ids=true | all-gather | bytes 612 | tf_op jit(solution)/shard_map/all_gather | solution.py:34
  142.7 0.1 constant_dynamic-slice_fusion.1
  142.8 0.1 copy.49
  142.9 0.1 copy.50
  142.9 0.0 copy-done.2
  142.9 0.6 dynamic-slice.2
  144.2 0.1 fusion.13
  144.5 0.0 all-to-all-done.1
  144.5 0.5 fusion.11
  145.0 0.2 fusion.12
  145.2 3.0 %convolution_multiply_fusion.1 = f32[48,4096]{1,0:T(8,128)S(1)} fusion(bf16[512,4096]{1,0:T(8,128)(2,1)} %param.11, f32[48]{0:T(128)S(1)} %fusion.13, bf16[4,6,8,128]{3,2,1,0:T(8,128)(2,1)S(1)} %fusion.12), kind=kOutput, calls=%fused_computation.17 | convolution fusion | flops 201523200 | bytes 5030080 | tf_op jit(solution)/shard_map/dot_general | solution.py:76
  148.2 66.3 %all-reduce.2 = bf16[48,4096]{1,0:T(8,128)(2,1)S(1)} all-reduce(f32[48,4096]{1,0:T(8,128)S(1)} %convolution_multiply_fusion.1), channel_id=2, replica_groups=mesh['groups'=2,'seq'=16] {'seq'}, use_global_device_ids=true, to_apply=%region_7.8.clone | all-reduce | flops 196608 | bytes 1179648
  214.5 0.6 dynamic-slice_convert_fusion
  (36 shorter events, 0.6 us)
Async XLA Ops:
  40.2 53.0 %copy-start = (s32[3,3]{1,0:T(4,128)S(1)}, s32[3,3]{1,0:T(4,128)}, u32[]{:S(2)}) copy-start(s32[3,3]{1,0:T(4,128)} %param.12) | copy-start | bytes 112
  40.2 82.2 %copy-start.1 = (s32[3,3]{1,0:T(4,128)S(1)}, s32[3,3]{1,0:T(4,128)}, u32[]{:S(2)}) copy-start(s32[3,3]{1,0:T(4,128)} %param.13) | copy-start | bytes 112
  40.2 102.7 %copy-start.2 = (u32[32]{0:T(128)S(1)}, u32[32]{0:T(128)}, u32[]{:S(2)}) copy-start(u32[32]{0:T(128)} %constant.70) | copy-start | bytes 388
  70.3 10.1 %all-to-all-start.2 = ((bf16[64,1,48]{2,1,0:T(2,128)(2,1)}), bf16[64,1,48]{2,1,0:T(2,128)(2,1)S(1)}, u32[]{:S(2)}, u32[]{:S(2)}) async-start(bf16[64,1,48]{2,1,0:T(2,128)(2,1)} %copy.39), calls=%async_computation.2 | async-start | bytes 65536 | tf_op jit(solution)/shard_map/all_to_all | solution.py:52
  89.6 54.9 %all-to-all-start.1 = ((bf16[64,1,48,128]{3,2,1,0:T(8,128)(2,1)}), bf16[64,1,48,128]{3,2,1,0:T(8,128)(2,1)S(1)}, u32[]{:S(2)}, u32[]{:S(2)}) async-start(bf16[64,1,48,128]{3,2,1,0:T(8,128)(2,1)} %bitcast.20), calls=%async_computation.1 | async-start | bytes 1572864 | tf_op jit(solution)/shard_map/all_to_all | solution.py:46
where the time goes:
time: 217 us; the launch traced here: 215 us
  blocking collectives  151 us (70%)
  matrix products  30.3 us (14%)
  local copies, waits for them, and re-layouts  16.7 us (8%)
  starting transfers between devices  7.11 us (3%)
  waiting for transfers between devices  6.56 us (3%)
  other arithmetic  2.41 us (1%)
    unnamed x1, blocking collectives  66.3 us
    all_gather x1, blocking collectives, on_device(): lax.all_gather(levels, 'seq', axis=1, tiled=True)  29.1 us
    all_gather x1, blocking collectives, on_device(): gathered = lax.all_gather(queries, 'seq', axis=0, tiled=True)  26.3 us
    all_gather x1, blocking collectives, on_device(): lax.all_gather(owner_map, 'seq', axis=1, tiled=True)  20.2 us
    dot_general x8, matrix products, local_block(): jnp.einsum('pqk,kph->pqh', expo.astype(jnp.bfloat16), value_block, prefer...  16.2 us
    unnamed x17, local copies, waits for them, and re-layouts  13.8 us
    dot_general x8, matrix products, local_block(): jnp.einsum('qph,kph->pqk', query_block, key_block, preferred_element_type...  10.7 us
    all_to_all x1, blocking collectives, on_device(): lax.all_to_all(peak[:, None].astype(jnp.bfloat16), 'seq', split_axis=0, c...  9.19 us
  transfers between devices with their start and end apart: 2, of which 1 were waited for; matrix products, arithmetic and copies ran while one was open for 1% of the time, Pallas kernels for 0%

commit v1 on v0

v1 whole, which is shorter than its diff:
```python
import functools
import math

import jax
import jax.numpy as jnp
from jax import lax
from jax.experimental import pallas as pl
from jax.experimental.pallas import tpu as pltpu
from jax.sharding import PartitionSpec as P

HD = 128
HEADS = 16
CONTROLS = 3
LEVELS = 8
SUB = 16
MESH = pl.DeviceIdType.MESH
F32 = jnp.float32
BF16 = jnp.bfloat16


def kernel(
    cfg, q_ref, k_hbm, v_hbm, w_hbm, out_ref,
    k_ref, v_ref, w_ref, qg, qf, qh,
    sb_core, rb_core, sb_y, rb_y, sb_z, rb_z,
    pf, pb, rc, sy, ry, sz, rz,
    load_sem, ag_send, ag_recv,
    core_s, core_r, y_s, y_r, z_s, z_r,
    pc_s, pc_r, py_s, py_r, pz_s, pz_r,
):
    n, outer, tokens_dev, heads_dev, pairs, block_rows, chunks = cfg
    tokens = tokens_dev * n
    group = lax.axis_index("groups")
    me = lax.axis_index("seq")
    z, y, c = me // 4, (me // 2) % 2, me % 2

    def dev(zz, yy, cc):
        return (group, zz * 4 + yy * 2 + cc)

    sibling, across = dev(z, y, 1 - c), dev(z, 1 - y, c)

    loads = [
        pltpu.make_async_copy(k_hbm, k_ref, load_sem.at[0]),
        pltpu.make_async_copy(v_hbm, v_ref, load_sem.at[1]),
        pltpu.make_async_copy(w_hbm, w_ref, load_sem.at[2]),
    ]
    for load in loads:
        load.start()

    barrier = pltpu.get_barrier_semaphore()
    pl.semaphore_signal(barrier, inc=1, device_id=sibling, device_id_type=MESH)
    pl.semaphore_signal(barrier, inc=1, device_id=across, device_id_type=MESH)
    for step in range(1, outer):
        pl.semaphore_signal(
            barrier, inc=1, device_id=dev((z + step) % outer, y, c), device_id_type=MESH
        )
    pl.semaphore_wait(barrier, outer + 1)

    def send(src, dst, s_sem, r_sem, target):
        return pltpu.make_async_remote_copy(
            src_ref=src, dst_ref=dst, send_sem=s_sem, recv_sem=r_sem,
            device_id=target, device_id_type=MESH,
        )

    def ag(block, slot, target, own=False):
        src = q_ref if own else qg.at[block]
        return send(src, qg.at[block], ag_send.at[slot], ag_recv.at[block], target)

    for step in range(1, outer):
        ag(me, step, dev((z + step) % outer, y, c), own=True).start()
    ag(me, outer, across, own=True).start()
    ag(me, 2 * outer, sibling, own=True).start()

    def widen(block):
        qf[pl.ds(pl.multiple_of(block * block_rows, SUB), block_rows), :] = qg[block].astype(F32)

    qf[pl.ds(pl.multiple_of(me * block_rows, SUB), block_rows), :] = q_ref[...].astype(F32)

    for step in range(1, outer):
        block = ((z + step) % outer) * 4 + y * 2 + c
        ag(block, step, across).wait_recv()
        ag(block, outer + step, across).start()
        ag(block, 2 * outer + step, sibling).start()
        widen(block)
    for step in range(outer):
        block = ((z + step) % outer) * 4 + (1 - y) * 2 + c
        ag(block, step, across).wait_recv()
        ag(block, 3 * outer + step, sibling).start()
        widen(block)
    for yy in (y, 1 - y):
        for step in range(outer):
            block = ((z + step) % outer) * 4 + yy * 2 + (1 - c)
            ag(block, step, sibling).wait_recv()
            widen(block)

    def token_rows(first):
        return jnp.concatenate(
            [qf[pl.ds(first(r), n, stride=block_rows), :] for r in range(tokens_dev)], axis=0
        )

    for h in range(pairs):
        qh[h] = token_rows(lambda r: r * pairs + h).astype(BF16)

    loads[0].wait()
    loads[1].wait()

    log_scale = HD ** -0.5 * math.log2(math.e)
    lane = lax.broadcasted_iota(jnp.int32, (tokens, HD), 1)

    def attend(target):
        parts = []
        for j in range(heads_dev):
            h = target * heads_dev + j
            cols = pl.ds(pl.multiple_of(h * HD, HD), HD)
            s = lax.dot_general(
                qh[h], k_ref[:, cols], (((1,), (1,)), ((), ())), preferred_element_type=F32
            ) * log_scale
            m = jnp.max(s, axis=1, keepdims=True).astype(BF16).astype(F32)
            p = jnp.exp2(s - m)
            total = jnp.sum(p, axis=1, keepdims=True)
            o = jnp.dot(p.astype(BF16), v_ref[:, cols], preferred_element_type=F32)
            parts.append((o, m, total))
        return parts

    def write(ref, parts):
        stat = jnp.zeros((tokens, HD), F32)
        for j, (o, m, total) in enumerate(parts):
            ref[j] = o.astype(BF16)
            stat = jnp.where(lane == 2 * j, m, stat)
            stat = jnp.where(lane == 2 * j + 1, total, stat)
        ref[heads_dev] = stat.astype(BF16)

    def merge(parts, refs):
        stats = [ref[heads_dev].astype(F32) for ref in refs]
        merged = []
        for j, (o, m, total) in enumerate(parts):
            ms = [stat[:, 2 * j:2 * j + 1] for stat in stats]
            best = functools.reduce(jnp.maximum, ms, m)
            f = jnp.exp2(m - best)
            o, total = o * f, total * f
            for ref, stat, mm in zip(refs, stats, ms):
                f = jnp.exp2(mm - best)
                o = o + ref[j].astype(F32) * f
                total = total + stat[:, 2 * j + 1:2 * j + 2] * f
            merged.append((o, best, total))
        return merged

    def core_copy(slot):
        return send(sb_core.at[slot], rb_core.at[slot], core_s.at[slot], core_r.at[slot], sibling)

    def y_copy(zz):
        return send(sb_y.at[zz], rb_y.at[zz], y_s.at[zz], y_r.at[zz], across)

    def z_copy(zz, sender):
        return send(sb_z.at[zz], rb_z.at[sender], z_s.at[zz], z_r.at[sender], dev(zz, y, c))

    def for_sibling(i, carry):
        zz = (z + 1 + i) % outer
        yy = (y + 1 + i // outer) % 2
        slot = zz * 2 + yy
        write(sb_core.at[slot], attend(slot * 2 + 1 - c))
        core_copy(slot).start()
        return carry

    lax.fori_loop(0, 2 * outer, for_sibling, 0)

    def for_across(i, carry):
        zz = (z + 1 + i) % outer
        slot = zz * 2 + 1 - y
        parts = attend(slot * 2 + c)
        core_copy(slot).wait_recv()
        write(sb_y.at[zz], merge(parts, [rb_core.at[slot]]))
        y_copy(zz).start()
        return carry

    lax.fori_loop(0, outer, for_across, 0)

    def for_z(i, carry):
        zz = (z + 1 + i) % outer
        slot = zz * 2 + y
        parts = attend(slot * 2 + c)
        core_copy(slot).wait_recv()
        y_copy(zz).wait_recv()
        write(sb_z.at[zz], merge(parts, [rb_core.at[slot], rb_y.at[zz]]))
        z_copy(zz, z).start()
        return carry

    lax.fori_loop(0, outer - 1, for_z, 0)

    parts = attend(me)
    core_copy(z * 2 + y).wait_recv()
    y_copy(z).wait_recv()
    parts = merge(parts, [rb_core.at[z * 2 + y], rb_y.at[z]])

    sections = pairs // HEADS
    section = me * heads_dev // HEADS
    info = jnp.zeros((tokens, HD), F32)
    for s in range(sections):
        rows = token_rows(lambda r: tokens_dev * pairs + r * sections + s)
        info = jnp.where(section == s, rows, info)
    place = info[:, 0:1].astype(jnp.int32)
    picked = lax.broadcasted_iota(jnp.int32, (tokens, tokens), 1) == place
    picked = picked.astype(F32).T.astype(BF16)
    level = jnp.broadcast_to(info[:, HD // 2:HD // 2 + 1], (tokens, HD)).astype(BF16)
    row_weight = jnp.dot(picked, level, preferred_element_type=F32)[:, 0:1] / LEVELS

    for step in range(1, outer):
        z_copy((z + step) % outer, (z + step) % outer).wait_recv()
    parts = merge(parts, [rb_z.at[(z + step) % outer] for step in range(1, outer)])
    attended = jnp.concatenate([(o / total).astype(BF16) for o, _, total in parts], axis=1)
    chosen = jnp.dot(picked, attended, preferred_element_type=F32).astype(BF16)

    loads[2].wait()
    half, quarter, piece = tokens // 2 * SUB, tokens // 4 * SUB, tokens_dev * SUB

    def rows_at(first, count):
        return pl.ds(pl.multiple_of(first, SUB), count)

    def pc_copy(cc):
        rows = rows_at((1 - c) * half, half)
        return send(pb.at[cc, rows], rc.at[cc], pc_s.at[cc], pc_r.at[cc], sibling)

    def py_copy(cc):
        return send(sy.at[cc], ry.at[cc], py_s.at[cc], py_r.at[cc], across)

    def pz_copy(cc, zz, sender):
        return send(
            sz.at[cc, zz], rz.at[cc, sender], pz_s.at[cc, zz], pz_r.at[cc, sender], dev(zz, y, c)
        )

    width = 4 * HD
    for cc in range(chunks):
        for g in range(SUB * HD // width):
            first = cc * SUB * HD + g * width
            product = jnp.dot(
                chosen, w_ref[:, first:first + width], preferred_element_type=F32
            ) * row_weight
            for t in range(width // HD):
                pf[cc, pl.ds(g * (width // HD) + t, tokens, stride=SUB), :] = (
                    product[:, t * HD:(t + 1) * HD]
                )
        rows = rows_at((1 - c) * half, half)
        pb[cc, rows] = pf[cc, rows].astype(BF16)
        pc_copy(cc).start()

    for cc in range(chunks):
        pc_copy(cc).wait_recv()
        away, near = rows_at((1 - y) * quarter, quarter), rows_at(y * quarter, quarter)
        away_own = rows_at(c * half + (1 - y) * quarter, quarter)
        sy[cc] = (pf[cc, away_own] + rc[cc, away].astype(F32)).astype(BF16)
        py_copy(cc).start()
    for cc in range(chunks):
        py_copy(cc).wait_recv()
        for step in range(1, outer):
            zz = (z + step) % outer
            own = rows_at(c * half + y * quarter + zz * piece, piece)
            from_core = rows_at(y * quarter + zz * piece, piece)
            from_y = rows_at(zz * piece, piece)
            sz[cc, zz] = (
                pf[cc, own] + rc[cc, from_core].astype(F32) + ry[cc, from_y].astype(F32)
            ).astype(BF16)
            pz_copy(cc, zz, z).start()
    for cc in range(chunks):
        own = rows_at(c * half + y * quarter + z * piece, piece)
        from_core = rows_at(y * quarter + z * piece, piece)
        from_y = rows_at(z * piece, piece)
        total = pf[cc, own] + rc[cc, from_core].astype(F32) + ry[cc, from_y].astype(F32)
        for step in range(1, outer):
            sender = (z + step) % outer
            pz_copy(cc, sender, sender).wait_recv()
            total = total + rz[cc, sender].astype(F32)
        out_ref[cc] = total.astype(BF16)

    for step in range(1, outer):
        ag(me, step, across).wait_send()
    for slot in range(outer, 4 * outer):
        ag(me, slot, across).wait_send()
    for slot in range(2 * outer):
        core_copy(slot).wait_send()
    for zz in range(outer):
        y_copy(zz).wait_send()
    for step in range(1, outer):
        z_copy((z + step) % outer, z).wait_send()
    for cc in range(chunks):
        pc_copy(cc).wait_send()
        py_copy(cc).wait_send()
        for step in range(1, outer):
            pz_copy(cc, (z + step) % outer, z).wait_send()


def on_device(queries, key_rows, value_rows, out_weight, levels, owner_map):
    n = lax.axis_size("seq")
    outer = n // 4
    tokens_dev, width = queries.shape
    pairs = width // HD
    heads_dev = out_weight.shape[0] // HD
    model = out_weight.shape[1]
    tokens = tokens_dev * n
    sections = pairs // HEADS
    keys = key_rows.shape[0]
    chunks = model // (SUB * HD)
    me = lax.axis_index("seq")

    own = me * tokens_dev + jnp.arange(tokens_dev, dtype=jnp.int32)
    base = jnp.concatenate([owner_map, own[None]], axis=0)
    holder, row = base // tokens_dev, base % tokens_dev
    order = (holder % 2) * (n // 2) + (holder // 2 % 2) * outer + holder // 4
    place = order * tokens_dev + row
    level = jnp.concatenate([levels, jnp.full((1, tokens_dev), LEVELS, jnp.int32)], axis=0)
    info = jnp.concatenate(
        [
            jnp.broadcast_to(place.T[..., None], (tokens_dev, sections, HD // 2)),
            jnp.broadcast_to(level.T[..., None], (tokens_dev, sections, HD // 2)),
        ],
        axis=2,
    ).reshape(tokens_dev * sections, HD).astype(BF16)
    used = tokens_dev * (pairs + sections)
    block_rows = -(-used // SUB) * SUB
    block = jnp.concatenate(
        [
            queries.reshape(tokens_dev * pairs, HD),
            info,
            jnp.zeros((block_rows - used, HD), BF16),
        ],
        axis=0,
    )

    cfg = (n, outer, tokens_dev, heads_dev, pairs, block_rows, chunks)
    message = (heads_dev + 1, tokens, HD)
    vmem = pltpu.VMEM
    dma = pltpu.SemaphoreType.DMA
    out = pl.pallas_call(
        functools.partial(kernel, cfg),
        out_shape=jax.ShapeDtypeStruct((chunks, tokens_dev * SUB, HD), BF16),
        in_specs=[pl.BlockSpec(memory_space=pltpu.VMEM)]
        + [pl.BlockSpec(memory_space=pl.ANY)] * 3,
        out_specs=pl.BlockSpec(memory_space=pltpu.VMEM),
        scratch_shapes=[
            vmem(key_rows.shape, BF16),
            vmem(value_rows.shape, BF16),
            vmem(out_weight.shape, BF16),
            vmem((n, block_rows, HD), BF16),
            vmem((n * block_rows, HD), F32),
            vmem((pairs, tokens, HD), BF16),
            vmem((n // 2,) + message, BF16),
            vmem((n // 2,) + message, BF16),
            vmem((outer,) + message, BF16),
            vmem((outer,) + message, BF16),
            vmem((outer,) + message, BF16),
            vmem((outer,) + message, BF16),
            vmem((chunks, tokens * SUB, HD), F32),
            vmem((chunks, tokens * SUB, HD), BF16),
            vmem((chunks, tokens // 2 * SUB, HD), BF16),
            vmem((chunks, tokens // 4 * SUB, HD), BF16),
            vmem((chunks, tokens // 4 * SUB, HD), BF16),
            vmem((chunks, outer, tokens_dev * SUB, HD), BF16),
            vmem((chunks, outer, tokens_dev * SUB, HD), BF16),
            dma((3,)),
            dma((4 * outer,)),
            dma((n,)),
            dma((n // 2,)),
            dma((n // 2,)),
            dma((outer,)),
            dma((outer,)),
            dma((outer,)),
            dma((outer,)),
            dma((chunks,)),
            dma((chunks,)),
            dma((chunks,)),
            dma((chunks,)),
            dma((chunks, outer)),
            dma((chunks, outer)),
        ],
        compiler_params=pltpu.CompilerParams(
            collective_id=0, has_side_effects=True, vmem_limit_bytes=56 * 1024 * 1024
        ),
        cost_estimate=pl.CostEstimate(
            flops=4 * tokens * keys * width + 2 * tokens * heads_dev * HD * model,
            bytes_accessed=2 * (2 * keys * width + heads_dev * HD * model),
            transcendentals=tokens * keys * pairs,
        ),
    )(block, key_rows, value_rows, out_weight)
    out = out.reshape(chunks, tokens_dev, SUB * HD)
    return out.transpose(1, 0, 2).reshape(tokens_dev, model)


def solution(mesh):
    return jax.shard_map(
        on_device,
        mesh=mesh,
        in_specs=(
            P(("groups", "seq"), None),
            P(("groups", "seq"), None),
            P(("groups", "seq"), None),
            P("seq", None),
            P(None, ("groups", "seq")),
            P(None, ("groups", "seq")),
        ),
        out_specs=P(("groups", "seq"), None),
        check_vma=False,
    )
```

time: 217 us -> 57.2 us (0.26)
  blocking collectives: 151 us -> 0 us
  Pallas kernels: 0 us -> 51.9 us
  matrix products: 30.3 us -> 0 us
  local copies, waits for them, and re-layouts: 16.7 us -> 2.76 us
  starting transfers between devices: 7.11 us -> 0 us
  waiting for transfers between devices: 6.56 us -> 0 us
    all_gather x3 -> x0, blocking collectives: 75.6 us -> none  [the longest x1 29.1 us: on_device(): lax.all_gather(levels, 'seq', axis=1, tiled=True)]
    unnamed x1 -> x0, blocking collectives: 66.3 us -> none
    pallas_call x0 -> x1, Pallas kernels: none -> 51.9 us  [on_device(): pl.pallas_call(functools.partial(kernel, cfg), out_shape=jax.ShapeDtypeSt...]
    dot_general x19 -> x0, matrix products: 30.3 us -> none  [the longest x8 16.2 us: local_block(): jnp.einsum('pqk,kph->pqh', expo.astype(jnp.bfloat16), value_block, prefer...]
    unnamed x17 -> x0, local copies, waits for them, and re-layouts: 13.8 us -> none
    all_to_all x1 -> x0, blocking collectives: 9.19 us -> none  [on_device(): lax.all_to_all(peak[:, None].astype(jnp.bfloat16), 'seq', split_axis=0, c...]
    all_to_all x2 -> x0, starting transfers between devices: 7.11 us -> none  [the longest x1 3.61 us: on_device(): lax.all_to_all(weighted[:, None].astype(jnp.bfloat16), 'seq', split_axis=...]
    all_to_all x2 -> x0, waiting for transfers between devices: 6.56 us -> none  [the longest x1 6.56 us: on_device(): lax.all_to_all(total[:, None].astype(jnp.bfloat16), 'seq', split_axis=0,...]
  transfers between devices with their start and end apart: 2 -> 0, of which waited for: 1 -> 0; matrix products, arithmetic and copies ran while one was open for 1% -> 0% of each run, Pallas kernels for 0% -> 0%
where the time goes in v1:
time: 57.2 us; the launch traced here: 56.9 us
  Pallas kernels  51.9 us (91%)
  local copies, waits for them, and re-layouts  2.76 us (5%)
  other arithmetic  2.21 us (4%)
    pallas_call x1, Pallas kernels, on_device(): pl.pallas_call(functools.partial(kernel, cfg), out_shape=jax.ShapeDtypeSt...  51.9 us
    another operation x2, other arithmetic  1.41 us
    reshape x1, local copies, waits for them, and re-layouts, on_device(): out = out.reshape(chunks, tokens_dev, SUB * HD)  1.37 us

profile of v1, /device:TPU:0, one launch (start us, length us, event | category | flops | bytes accessed | tf_op | source)
XLA Modules:
  0.0 56.9 jit_solution(17849169070335145834)
XLA Ops:
  0.0 0.7 %fusion.12 = bf16[3,4]{0,1:T(4,128)(2,1)S(1)} fusion(s32[1,3]{1,0:T(1,128)S(1)} %iota_add_fusion, s32[3,3]{1,0:T(4,128)} %param.11), kind=kLoop, calls=%fused_computation.31 | loop fusion | flops 720 | bytes 72 | tf_op jit(solution)/shard_map/convert.2
  0.7 0.1 copy.10
  0.8 0.1 pad.3.clone
  0.9 0.7 %fusion.11 = bf16[3,4]{0,1:T(4,128)(2,1)S(1)} fusion(s32[3,3]{1,0:T(4,128)} %param.10), kind=kLoop, calls=%fused_computation.30 | loop fusion | flops 12 | bytes 60 | tf_op jit(solution)/shard_map/convert.3
  1.6 0.1 copy.11
  1.7 0.1 broadcast_in_dim.7
  1.8 0.1 broadcast_in_dim.6
  1.9 0.1 pad_maximum_fusion
  2.0 0.9 %reshape.20 = bf16[192,128]{1,0:T(8,128)(2,1)S(1)} reshape(bf16[3,8192]{1,0:T(4,128)(2,1)} %param.6) | data formatting | bytes 98304 | tf_op jit(solution)/shard_map/reshape | solution.py:320
  2.9 0.7 %maximum_maximum_fusion.q_ref = bf16[208,128]{1,0:T(8,128)(2,1)} fusion(bf16[12,128]{1,0:T(8,128)(2,1)S(1)} %convert_element_type.4, bf16[192,128]{1,0:T(8,128)(2,1)S(1)} %reshape.20, bf16[208]{0:T(256)(128)(2,1)S(1)} %pad.3.clone), kind=kLoop, calls=%fused_computation | loop fusion | flops 159744 | bytes 105888 | tf_op jit(solution)/shard_map/concatenate | solution.py:318
  3.6 51.9 %shard_map.64 = bf16[2,48,128]{2,1,0:T(8,128)(2,1)} custom-call(bf16[208,128]{1,0:T(8,128)(2,1)} %maximum_maximum_fusion.q_ref, bf16[256,8192]{1,0:T(8,128)(2,1)} %k_hbm.1, bf16[256,8192]{1,0:T(8,128)(2,1)} %v_hbm.1, bf16[512,4096]{1,0:T(8,128)(2,1)} %w_hbm.1), custom_call_target="tpu_custom_call" | custom-call | flops 603979776 | bytes 12582912 | tf_op jit(solution)/shard_map/pallas_call | solution.py:331
  55.5 1.4 %reshape.21 = bf16[2,3,2048]{2,1,0:T(4,128)(2,1)} reshape(bf16[2,48,128]{2,1,0:T(8,128)(2,1)} %shard_map.64) | data formatting | bytes 49152 | tf_op jit(solution)/shard_map/reshape | solution.py:382
  (3 shorter events, 0.0 us)

commit v2 on v1

v2 whole, which is shorter than its diff:
```python
import functools
import math

import jax
import jax.numpy as jnp
from jax import lax
from jax.experimental import pallas as pl
from jax.experimental.pallas import tpu as pltpu
from jax.sharding import PartitionSpec as P

HD = 128
HEADS = 16
CONTROLS = 3
LEVELS = 8
SUB = 16
MESH = pl.DeviceIdType.MESH
F32 = jnp.float32
BF16 = jnp.bfloat16


def kernel(
    cfg, q_hbm, k_hbm, v_hbm, w_hbm, level_hbm, owner_hbm, out_ref,
    k_ref, v_ref, w_ref, q_ref, level_ref, owner_ref, qs, qg, qf, qh,
    sb_core, rb_core, sb_y, rb_y, sb_z, rb_z,
    pf, pb, rc, sy, ry, sz, rz, done,
    load_sem, ag_send, ag_recv,
    core_s, core_r, y_s, y_r, z_s, z_r,
    pc_s, pc_r, py_s, py_r, pz_s, pz_r,
):
    n, outer, tokens_dev, heads_dev, pairs, chunks = cfg
    tokens = tokens_dev * n
    group = lax.axis_index("groups")
    me = lax.axis_index("seq")
    z, y, c = me // 4, (me // 2) % 2, me % 2

    def dev(zz, yy, cc):
        return (group, zz * 4 + yy * 2 + cc)

    sibling, across = dev(z, y, 1 - c), dev(z, 1 - y, c)

    loads = [
        pltpu.make_async_copy(src, dst, load_sem.at[i])
        for i, (src, dst) in enumerate(
            [
                (q_hbm, q_ref), (level_hbm, level_ref), (owner_hbm, owner_ref),
                (k_hbm, k_ref), (v_hbm, v_ref), (w_hbm, w_ref),
            ]
        )
    ]
    for load in loads:
        load.start()

    barrier = pltpu.get_barrier_semaphore()
    pl.semaphore_signal(barrier, inc=1, device_id=sibling, device_id_type=MESH)
    pl.semaphore_signal(barrier, inc=1, device_id=across, device_id_type=MESH)
    for step in range(1, outer):
        pl.semaphore_signal(
            barrier, inc=1, device_id=dev((z + step) % outer, y, c), device_id_type=MESH
        )

    def send(src, dst, s_sem, r_sem, target):
        return pltpu.make_async_remote_copy(
            src_ref=src, dst_ref=dst, send_sem=s_sem, recv_sem=r_sem,
            device_id=target, device_id_type=MESH,
        )

    part_heads = pairs // 2
    part_rows = tokens_dev * part_heads
    block_rows = 2 * part_rows + SUB
    for load in loads[:3]:
        load.wait()
    for h in range(pairs):
        first = h // part_heads * part_rows + h % part_heads
        qs[pl.ds(first, tokens_dev, stride=part_heads), :] = (
            q_ref[:, h * HD:(h + 1) * HD].astype(F32)
        )
    qs[2 * part_rows:, :] = jnp.zeros((SUB, HD), F32)
    qs[2 * part_rows:2 * part_rows + CONTROLS, 0:tokens_dev] = owner_ref[...].astype(F32)
    qs[2 * part_rows + 8:2 * part_rows + 8 + CONTROLS, 0:tokens_dev] = level_ref[...].astype(F32)
    qg[me] = qs[...].astype(BF16)
    qf[pl.ds(pl.multiple_of(me * block_rows, SUB), block_rows), :] = qs[...]

    pl.semaphore_wait(barrier, outer + 1)

    spans = (pl.ds(0, part_rows), pl.ds(part_rows, part_rows + SUB))

    def ag(part, block, slot, target):
        ref = qg.at[block, spans[part]]
        return send(ref, ref, ag_send.at[part, slot], ag_recv.at[part, block], target)

    for part in range(2):
        for step in range(1, outer):
            ag(part, me, step, dev((z + step) % outer, y, c)).start()
        ag(part, me, outer, across).start()
        ag(part, me, 2 * outer, sibling).start()

    def widen(part, block):
        first = block * block_rows + part * part_rows
        count = part_rows + part * SUB
        qf[pl.ds(pl.multiple_of(first, SUB), count), :] = qg[block, spans[part]].astype(F32)

    def from_z(part):
        for step in range(1, outer):
            block = ((z + step) % outer) * 4 + y * 2 + c
            ag(part, block, step, across).wait_recv()
            ag(part, block, outer + step, across).start()
            ag(part, block, 2 * outer + step, sibling).start()
            widen(part, block)

    def from_across(part, step):
        block = ((z + step) % outer) * 4 + (1 - y) * 2 + c
        ag(part, block, step, across).wait_recv()
        ag(part, block, 3 * outer + step, sibling).start()
        widen(part, block)

    def from_sibling(part):
        for yy in (y, 1 - y):
            for step in range(outer):
                block = ((z + step) % outer) * 4 + yy * 2 + (1 - c)
                ag(part, block, step, sibling).wait_recv()
                widen(part, block)
        for h in range(part_heads):
            qh[part * part_heads + h] = jnp.concatenate(
                [
                    qf[pl.ds(part * part_rows + r * part_heads + h, n, stride=block_rows), :]
                    for r in range(tokens_dev)
                ],
                axis=0,
            ).astype(BF16)

    from_z(0)
    for step in range(outer):
        from_across(0, step)
    from_z(1)
    from_sibling(0)
    loads[3].wait()
    loads[4].wait()

    log_scale = HD ** -0.5 * math.log2(math.e)
    lane = lax.broadcasted_iota(jnp.int32, (tokens, HD), 1)
    mid = HD // 2

    def attend(targets):
        heads = [t * heads_dev + j for t in targets for j in range(heads_dev)]
        cols = [pl.ds(pl.multiple_of(h * HD, HD), HD) for h in heads]
        scores = [
            lax.dot_general(
                qh[h], k_ref[:, col], (((1,), (1,)), ((), ())), preferred_element_type=F32
            ) * log_scale
            for h, col in zip(heads, cols)
        ]
        peaks = [jnp.max(s, axis=1, keepdims=True).astype(BF16).astype(F32) for s in scores]
        expo = [jnp.exp2(s - m) for s, m in zip(scores, peaks)]
        totals = [jnp.sum(p, axis=1, keepdims=True) for p in expo]
        sums = [
            jnp.dot(p.astype(BF16), v_ref[:, col], preferred_element_type=F32)
            for p, col in zip(expo, cols)
        ]
        found = []
        for i in range(len(targets)):
            stat = jnp.zeros((tokens, HD), F32)
            for j in range(heads_dev):
                stat = jnp.where(lane == j, peaks[i * heads_dev + j], stat)
                stat = jnp.where(lane == mid + j, totals[i * heads_dev + j], stat)
            found.append((sums[i * heads_dev:(i + 1) * heads_dev], stat))
        return found

    def write(ref, found):
        sums, stat = found
        for j in range(heads_dev):
            ref[j] = sums[j].astype(BF16)
        ref[heads_dev] = stat.astype(BF16)

    def merge(found, refs):
        sums, stat = found
        stats = [stat] + [ref[heads_dev].astype(F32) for ref in refs]
        best = functools.reduce(jnp.maximum, stats)
        factors = [jnp.exp2(s - best) for s in stats]
        total = sum(s * pltpu.roll(f, mid, 1) for s, f in zip(stats, factors))
        merged = []
        for j in range(heads_dev):
            o = sums[j] * factors[0][:, j:j + 1]
            for ref, f in zip(refs, factors[1:]):
                o = o + ref[j].astype(F32) * f[:, j:j + 1]
            merged.append(o)
        return merged, jnp.where(lane < mid, best, total)

    def core_copy(slot):
        return send(sb_core.at[slot], rb_core.at[slot], core_s.at[slot], core_r.at[slot], sibling)

    def y_copy(zz):
        return send(sb_y.at[zz], rb_y.at[zz], y_s.at[zz], y_r.at[zz], across)

    def z_copy(zz, sender):
        return send(sb_z.at[zz], rb_z.at[sender], z_s.at[zz], z_r.at[sender], dev(zz, y, c))

    def sibling_slots(zz):
        slots = [zz * 2 + 1 - y, zz * 2 + y]
        for slot, found in zip(slots, attend([slot * 2 + 1 - c for slot in slots])):
            write(sb_core.at[slot], found)
            core_copy(slot).start()

    def first_half(i, carry):
        sibling_slots(i)
        from_across(1, 2 * i)
        from_across(1, 2 * i + 1)
        return carry

    def second_half(i, carry):
        sibling_slots(outer // 2 + i)
        return carry

    lax.fori_loop(0, outer // 2, first_half, 0)
    from_sibling(1)
    lax.fori_loop(0, outer // 2, second_half, 0)

    def for_across(i, carry):
        zs = [(z + 1 + 2 * i) % outer, (z + 2 + 2 * i) % outer]
        slots = [zz * 2 + 1 - y for zz in zs]
        both = attend([slot * 2 + c for slot in slots])
        for zz, slot, found in zip(zs, slots, both):
            core_copy(slot).wait_recv()
            write(sb_y.at[zz], merge(found, [rb_core.at[slot]]))
            y_copy(zz).start()
        return carry

    lax.fori_loop(0, outer // 2, for_across, 0)

    def collect(zz, found):
        slot = zz * 2 + y
        core_copy(slot).wait_recv()
        y_copy(zz).wait_recv()
        return merge(found, [rb_core.at[slot], rb_y.at[zz]])

    def for_z(i, carry):
        zs = [(z + 1 + 2 * i) % outer, (z + 2 + 2 * i) % outer]
        for zz, found in zip(zs, attend([zz * 4 + y * 2 + c for zz in zs])):
            write(sb_z.at[zz], collect(zz, found))
            z_copy(zz, z).start()
        return carry

    lax.fori_loop(0, outer // 2 - 1, for_z, 0)
    final = (z + outer - 1) % outer
    found, mine = attend([final * 4 + y * 2 + c, me])
    write(sb_z.at[final], collect(final, found))
    z_copy(final, z).start()
    mine = collect(z, mine)

    section = me * heads_dev // HEADS

    def column(first):
        rows = jnp.zeros((n, HD), F32)
        for s in range(CONTROLS):
            found_rows = qf[pl.ds(2 * part_rows + first + s, n, stride=block_rows), :]
            rows = jnp.where(section == s, found_rows, rows)
        return jnp.concatenate([rows[:, r:r + 1] for r in range(tokens_dev)], axis=0)

    position = lax.broadcasted_iota(jnp.int32, (n, 1), 0) * tokens_dev
    position = jnp.concatenate([position + r for r in range(tokens_dev)], axis=0).astype(F32)
    is_base = section >= CONTROLS
    owner = jnp.where(is_base, position, column(0))
    level = jnp.where(is_base, float(LEVELS), column(8))
    holder = jnp.floor((owner + 0.5) * (1.0 / tokens_dev))
    chip = jnp.floor(holder * 0.5)
    z_of = jnp.floor(holder * 0.25)
    order = (holder - 2 * chip) * (n // 2) + (chip - 2 * z_of) * outer + z_of
    place = order * tokens_dev + owner - holder * tokens_dev
    picked = lax.broadcasted_iota(jnp.int32, (tokens, tokens), 1) == place.astype(jnp.int32)
    picked = picked.astype(F32).T.astype(BF16)
    level = jnp.broadcast_to(level, (tokens, HD)).astype(BF16)
    row_weight = jnp.dot(picked, level, preferred_element_type=F32)[:, 0:1] / LEVELS

    for step in range(1, outer):
        z_copy((z + step) % outer, (z + step) % outer).wait_recv()
    sums, stat = merge(mine, [rb_z.at[(z + step) % outer] for step in range(1, outer)])
    attended = jnp.concatenate(
        [(sums[j] / stat[:, mid + j:mid + j + 1]).astype(BF16) for j in range(heads_dev)], axis=1
    )
    chosen = jnp.dot(picked, attended, preferred_element_type=F32).astype(BF16)

    loads[5].wait()
    half, quarter, piece = tokens // 2 * SUB, tokens // 4 * SUB, tokens_dev * SUB

    def rows_at(first, count):
        return pl.ds(pl.multiple_of(first, SUB), count)

    def pc_copy(cc):
        rows = rows_at((1 - c) * half, half)
        return send(pb.at[cc, rows], rc.at[cc], pc_s.at[cc], pc_r.at[cc], sibling)

    def py_copy(cc):
        return send(sy.at[cc], ry.at[cc], py_s.at[cc], py_r.at[cc], across)

    def pz_copy(cc, zz, sender):
        return send(
            sz.at[cc, zz], rz.at[cc, sender], pz_s.at[cc, zz], pz_r.at[cc, sender], dev(zz, y, c)
        )

    width = 4 * HD
    for cc in range(chunks):
        for g in range(SUB * HD // width):
            first = cc * SUB * HD + g * width
            product = jnp.dot(
                chosen, w_ref[:, first:first + width], preferred_element_type=F32
            ) * row_weight
            for t in range(width // HD):
                pf[cc, pl.ds(g * (width // HD) + t, tokens, stride=SUB), :] = (
                    product[:, t * HD:(t + 1) * HD]
                )
        rows = rows_at((1 - c) * half, half)
        pb[cc, rows] = pf[cc, rows].astype(BF16)
        pc_copy(cc).start()

    for cc in range(chunks):
        pc_copy(cc).wait_recv()
        away, near = rows_at((1 - y) * quarter, quarter), rows_at(y * quarter, quarter)
        away_own = rows_at(c * half + (1 - y) * quarter, quarter)
        sy[cc] = (pf[cc, away_own] + rc[cc, away].astype(F32)).astype(BF16)
        py_copy(cc).start()
    for cc in range(chunks):
        py_copy(cc).wait_recv()
        for step in range(1, outer):
            zz = (z + step) % outer
            own = rows_at(c * half + y * quarter + zz * piece, piece)
            from_core = rows_at(y * quarter + zz * piece, piece)
            from_y = rows_at(zz * piece, piece)
            sz[cc, zz] = (
                pf[cc, own] + rc[cc, from_core].astype(F32) + ry[cc, from_y].astype(F32)
            ).astype(BF16)
            pz_copy(cc, zz, z).start()
    for cc in range(chunks):
        own = rows_at(c * half + y * quarter + z * piece, piece)
        from_core = rows_at(y * quarter + z * piece, piece)
        from_y = rows_at(z * piece, piece)
        total = pf[cc, own] + rc[cc, from_core].astype(F32) + ry[cc, from_y].astype(F32)
        for step in range(1, outer):
            sender = (z + step) % outer
            pz_copy(cc, sender, sender).wait_recv()
            total = total + rz[cc, sender].astype(F32)
        done[...] = total
        for t in range(SUB):
            out_ref[:, (cc * SUB + t) * HD:(cc * SUB + t + 1) * HD] = (
                done[pl.ds(t, tokens_dev, stride=SUB), :].astype(BF16)
            )

    for part in range(2):
        for slot in range(1, 4 * outer):
            ag(part, me, slot, across).wait_send()
    for slot in range(2 * outer):
        core_copy(slot).wait_send()
    for zz in range(outer):
        y_copy(zz).wait_send()
    for step in range(1, outer):
        z_copy((z + step) % outer, z).wait_send()
    for cc in range(chunks):
        pc_copy(cc).wait_send()
        py_copy(cc).wait_send()
        for step in range(1, outer):
            pz_copy(cc, (z + step) % outer, z).wait_send()


def on_device(queries, key_rows, value_rows, out_weight, levels, owner_map):
    n = lax.axis_size("seq")
    outer = n // 4
    tokens_dev, width = queries.shape
    pairs = width // HD
    heads_dev = out_weight.shape[0] // HD
    model = out_weight.shape[1]
    tokens = tokens_dev * n
    keys = key_rows.shape[0]
    chunks = model // (SUB * HD)
    block_rows = tokens_dev * pairs + SUB

    cfg = (n, outer, tokens_dev, heads_dev, pairs, chunks)
    message = (heads_dev + 1, tokens, HD)
    vmem = pltpu.VMEM
    dma = pltpu.SemaphoreType.DMA
    return pl.pallas_call(
        functools.partial(kernel, cfg),
        out_shape=jax.ShapeDtypeStruct((tokens_dev, model), BF16),
        in_specs=[pl.BlockSpec(memory_space=pl.ANY)] * 6,
        out_specs=pl.BlockSpec(memory_space=pltpu.VMEM),
        scratch_shapes=[
            vmem(key_rows.shape, BF16),
            vmem(value_rows.shape, BF16),
            vmem(out_weight.shape, BF16),
            vmem(queries.shape, BF16),
            vmem(levels.shape, jnp.int32),
            vmem(owner_map.shape, jnp.int32),
            vmem((block_rows, HD), F32),
            vmem((n, block_rows, HD), BF16),
            vmem((n * block_rows, HD), F32),
            vmem((pairs, tokens, HD), BF16),
            vmem((n // 2,) + message, BF16),
            vmem((n // 2,) + message, BF16),
            vmem((outer,) + message, BF16),
            vmem((outer,) + message, BF16),
            vmem((outer,) + message, BF16),
            vmem((outer,) + message, BF16),
            vmem((chunks, tokens * SUB, HD), F32),
            vmem((chunks, tokens * SUB, HD), BF16),
            vmem((chunks, tokens // 2 * SUB, HD), BF16),
            vmem((chunks, tokens // 4 * SUB, HD), BF16),
            vmem((chunks, tokens // 4 * SUB, HD), BF16),
            vmem((chunks, outer, tokens_dev * SUB, HD), BF16),
            vmem((chunks, outer, tokens_dev * SUB, HD), BF16),
            vmem((tokens_dev * SUB, HD), F32),
            dma((6,)),
            dma((2, 4 * outer)),
            dma((2, n)),
            dma((n // 2,)),
            dma((n // 2,)),
            dma((outer,)),
            dma((outer,)),
            dma((outer,)),
            dma((outer,)),
            dma((chunks,)),
            dma((chunks,)),
            dma((chunks,)),
            dma((chunks,)),
            dma((chunks, outer)),
            dma((chunks, outer)),
        ],
        compiler_params=pltpu.CompilerParams(
            collective_id=0, has_side_effects=True, vmem_limit_bytes=56 * 1024 * 1024
        ),
        cost_estimate=pl.CostEstimate(
            flops=4 * tokens * keys * width + 2 * tokens * heads_dev * HD * model,
            bytes_accessed=2 * (2 * keys * width + heads_dev * HD * model),
            transcendentals=tokens * keys * pairs,
        ),
    )(queries, key_rows, value_rows, out_weight, levels, owner_map)


def solution(mesh):
    return jax.shard_map(
        on_device,
        mesh=mesh,
        in_specs=(
            P(("groups", "seq"), None),
            P(("groups", "seq"), None),
            P(("groups", "seq"), None),
            P("seq", None),
            P(None, ("groups", "seq")),
            P(None, ("groups", "seq")),
        ),
        out_specs=P(("groups", "seq"), None),
        check_vma=False,
    )
```

time: 57.2 us -> 44.2 us (0.77)
  Pallas kernels: 51.9 us -> 42.6 us
  other arithmetic: 2.21 us -> 0 us
  local copies, waits for them, and re-layouts: 2.76 us -> 1.39 us
    pallas_call x1, Pallas kernels: 51.9 us -> 42.6 us  [on_device(): pl.pallas_call(functools.partial(kernel, cfg), out_shape=jax.ShapeDtypeSt...]
    reshape x2 -> x0, local copies, waits for them, and re-layouts: 2.29 us -> none  [the longest x1 1.37 us: on_device(): out = out.reshape(chunks, tokens_dev, SUB * HD)]
    another operation x2 -> x0, other arithmetic: 1.41 us -> none
    unnamed x0 -> x1, local copies, waits for them, and re-layouts: none -> 1.39 us
    concatenate x2 -> x0, other arithmetic: 0.8 us -> none  [the longest x1 0.72 us: on_device(): jnp.concatenate([queries.reshape(tokens_dev * pairs, HD), info, jnp.zeros...]
where the time goes in v2:
time: 44.2 us; the launch traced here: 44 us
  Pallas kernels  42.6 us (96%)
  local copies, waits for them, and re-layouts  1.39 us (3%)
    pallas_call x1, Pallas kernels, on_device(): pl.pallas_call(functools.partial(kernel, cfg), out_shape=jax.ShapeDtypeSt...  42.6 us
    unnamed x1, local copies, waits for them, and re-layouts  1.39 us

profile of v2, /device:TPU:0, one launch (start us, length us, event | category | flops | bytes accessed | tf_op | source)
XLA Modules:
  0.0 44.0 jit_solution(12642972113406721874)
XLA Ops:
  0.0 42.6 %shard_map.64 = bf16[3,4096]{1,0:T(4,128)(2,1)} custom-call(bf16[3,8192]{1,0:T(4,128)(2,1)} %q_hbm.1, bf16[256,8192]{1,0:T(8,128)(2,1)} %k_hbm.1, bf16[256,8192]{1,0:T(8,128)(2,1)} %v_hbm.1, bf16[512,4096]{1,0:T(8,128)(2,1)} %w_hbm.1, s32[3,3]{1,0:T(4,128)} %level_hbm.1, s32[3,3]{1,0:T(4,128)} %owner_hbm.1), custom_call_target="tpu_custom_call" | custom-call | flops 603979776 | bytes 12582912 | tf_op jit(solution)/shard_map/pallas_call | solution.py:378
  42.7 1.4 %copy.8 = bf16[3,4096]{1,0:T(4,128)(2,1)} copy(bf16[3,4096]{1,0:T(4,128)(2,1)} %shard_map.64) | data formatting | bytes 49152

commit v3 on v2

--- a/solution.py
+++ b/solution.py
@@ -47,7 +47,7 @@
             ]
         )
     ]
-    for load in loads:
+    for load in loads[:5]:
         load.start()
 
     barrier = pltpu.get_barrier_semaphore()
@@ -132,6 +132,7 @@
     for step in range(outer):
         from_across(0, step)
     from_z(1)
+    loads[5].start()
     from_sibling(0)
     loads[3].wait()
     loads[4].wait()
@@ -143,19 +144,27 @@
     def attend(targets):
         heads = [t * heads_dev + j for t in targets for j in range(heads_dev)]
         cols = [pl.ds(pl.multiple_of(h * HD, HD), HD) for h in heads]
-        scores = [
-            lax.dot_general(
-                qh[h], k_ref[:, col], (((1,), (1,)), ((), ())), preferred_element_type=F32
-            ) * log_scale
-            for h, col in zip(heads, cols)
-        ]
-        peaks = [jnp.max(s, axis=1, keepdims=True).astype(BF16).astype(F32) for s in scores]
-        expo = [jnp.exp2(s - m) for s, m in zip(scores, peaks)]
-        totals = [jnp.sum(p, axis=1, keepdims=True) for p in expo]
-        sums = [
-            jnp.dot(p.astype(BF16), v_ref[:, col], preferred_element_type=F32)
-            for p, col in zip(expo, cols)
-        ]
+        count = len(heads)
+        scores, expo = [None] * count, [None] * count
+        peaks, totals, sums = [None] * count, [None] * count, [None] * count
+        for step in range(count + 4):
+            if step < count:
+                scores[step] = lax.dot_general(
+                    qh[heads[step]], k_ref[:, cols[step]], (((1,), (1,)), ((), ())),
+                    preferred_element_type=F32,
+                )
+            i = step - 2
+            if 0 <= i < count:
+                peak = jnp.max(scores[i], axis=1, keepdims=True) * log_scale
+                peaks[i] = peak.astype(BF16).astype(F32)
+                p = jnp.exp2(scores[i] * log_scale - peaks[i])
+                totals[i] = jnp.sum(p, axis=1, keepdims=True)
+                expo[i] = p.astype(BF16)
+                scores[i] = None
+            i = step - 4
+            if 0 <= i < count:
+                sums[i] = jnp.dot(expo[i], v_ref[:, cols[i]], preferred_element_type=F32)
+                expo[i] = None
         found = []
         for i in range(len(targets)):
             stat = jnp.zeros((tokens, HD), F32)
@@ -195,24 +204,24 @@
         return send(sb_z.at[zz], rb_z.at[sender], z_s.at[zz], z_r.at[sender], dev(zz, y, c))
 
     def sibling_slots(zz):
-        slots = [zz * 2 + 1 - y, zz * 2 + y]
+        slots = [zz * 2 + 1 - y, zz * 2 + y, zz * 2 + 3 - y, zz * 2 + 2 + y]
         for slot, found in zip(slots, attend([slot * 2 + 1 - c for slot in slots])):
             write(sb_core.at[slot], found)
             core_copy(slot).start()
 
     def first_half(i, carry):
-        sibling_slots(i)
-        from_across(1, 2 * i)
-        from_across(1, 2 * i + 1)
+        sibling_slots(2 * i)
+        for step in range(4):
+            from_across(1, 4 * i + step)
         return carry
 
     def second_half(i, carry):
-        sibling_slots(outer // 2 + i)
+        sibling_slots(outer // 2 + 2 * i)
         return carry
 
-    lax.fori_loop(0, outer // 2, first_half, 0)
+    lax.fori_loop(0, outer // 4, first_half, 0)
     from_sibling(1)
-    lax.fori_loop(0, outer // 2, second_half, 0)
+    lax.fori_loop(0, outer // 4, second_half, 0)
 
     def for_across(i, carry):
         zs = [(z + 1 + 2 * i) % outer, (z + 2 + 2 * i) % outer]
@@ -340,7 +349,7 @@
         done[...] = total
         for t in range(SUB):
             out_ref[:, (cc * SUB + t) * HD:(cc * SUB + t + 1) * HD] = (
-                done[pl.ds(t, tokens_dev, stride=SUB), :].astype(BF16)
+                done[pl.ds(t, tokens_dev, stride=SUB), :]
             )
 
     for part in range(2):
@@ -377,7 +386,7 @@
     dma = pltpu.SemaphoreType.DMA
     return pl.pallas_call(
         functools.partial(kernel, cfg),
-        out_shape=jax.ShapeDtypeStruct((tokens_dev, model), BF16),
+        out_shape=jax.ShapeDtypeStruct((tokens_dev, model), F32),
         in_specs=[pl.BlockSpec(memory_space=pl.ANY)] * 6,
         out_specs=pl.BlockSpec(memory_space=pltpu.VMEM),
         scratch_shapes=[
@@ -429,7 +438,7 @@
             bytes_accessed=2 * (2 * keys * width + heads_dev * HD * model),
             transcendentals=tokens * keys * pairs,
         ),
-    )(queries, key_rows, value_rows, out_weight, levels, owner_map)
+    )(queries, key_rows, value_rows, out_weight, levels, owner_map).astype(BF16)
 
 
 def solution(mesh):

time: 44.2 us -> 44.3 us (level)
  other arithmetic: 0 us -> 1.47 us
  local copies, waits for them, and re-layouts: 1.39 us -> 0 us
    convert_element_type x0 -> x1, other arithmetic: none -> 1.47 us  [on_device(): return pl.pallas_call(functools.partial(kernel, cfg), out_shape=jax.Shape...]
    unnamed x1 -> x0, local copies, waits for them, and re-layouts: 1.39 us -> none
where the time goes in v3:
time: 44.3 us; the launch traced here: 44.2 us
  Pallas kernels  42.7 us (96%)
  other arithmetic  1.47 us (3%)
    pallas_call x1, Pallas kernels, on_device(): pl.pallas_call(functools.partial(kernel, cfg), out_shape=jax.ShapeDtypeSt...  42.7 us
    convert_element_type x1, other arithmetic, on_device(): return pl.pallas_call(functools.partial(kernel, cfg), out_shape=jax.Shape...  1.47 us

profile of v3, /device:TPU:0, one launch (start us, length us, event | category | flops | bytes accessed | tf_op | source)
XLA Modules:
  0.0 44.2 jit_solution(10261399264900517311)
XLA Ops:
  0.0 42.7 %shard_map.64 = f32[3,4096]{1,0:T(4,128)} custom-call(bf16[3,8192]{1,0:T(4,128)(2,1)} %q_hbm.1, bf16[256,8192]{1,0:T(8,128)(2,1)} %k_hbm.1, bf16[256,8192]{1,0:T(8,128)(2,1)} %v_hbm.1, bf16[512,4096]{1,0:T(8,128)(2,1)} %w_hbm.1, s32[3,3]{1,0:T(4,128)} %level_hbm.1, s32[3,3]{1,0:T(4,128)} %owner_hbm.1), custom_call_target="tpu_custom_call" | custom-call | flops 603979776 | bytes 12582912 | tf_op jit(solution)/shard_map/pallas_call | solution.py:387
  42.7 1.5 %convert_element_type.3 = bf16[3,4096]{1,0:T(4,128)(2,1)} convert(f32[3,4096]{1,0:T(4,128)} %shard_map.64) | non-fusion elementwise | flops 12288 | bytes 73728 | tf_op jit(solution)/shard_map/convert_element_type | solution.py:441

commit v4 on v3

--- a/solution.py
+++ b/solution.py
@@ -13,6 +13,7 @@
 CONTROLS = 3
 LEVELS = 8
 SUB = 16
+PARTS = 4
 MESH = pl.DeviceIdType.MESH
 F32 = jnp.float32
 BF16 = jnp.bfloat16
@@ -64,9 +65,10 @@
             device_id=target, device_id_type=MESH,
         )
 
-    part_heads = pairs // 2
+    part_heads = pairs // PARTS
     part_rows = tokens_dev * part_heads
-    block_rows = 2 * part_rows + SUB
+    info_at = PARTS * part_rows
+    block_rows = info_at + SUB
     for load in loads[:3]:
         load.wait()
     for h in range(pairs):
@@ -74,21 +76,22 @@
         qs[pl.ds(first, tokens_dev, stride=part_heads), :] = (
             q_ref[:, h * HD:(h + 1) * HD].astype(F32)
         )
-    qs[2 * part_rows:, :] = jnp.zeros((SUB, HD), F32)
-    qs[2 * part_rows:2 * part_rows + CONTROLS, 0:tokens_dev] = owner_ref[...].astype(F32)
-    qs[2 * part_rows + 8:2 * part_rows + 8 + CONTROLS, 0:tokens_dev] = level_ref[...].astype(F32)
+    qs[info_at:, :] = jnp.zeros((SUB, HD), F32)
+    qs[info_at:info_at + CONTROLS, 0:tokens_dev] = owner_ref[...].astype(F32)
+    qs[info_at + 8:info_at + 8 + CONTROLS, 0:tokens_dev] = level_ref[...].astype(F32)
     qg[me] = qs[...].astype(BF16)
     qf[pl.ds(pl.multiple_of(me * block_rows, SUB), block_rows), :] = qs[...]
 
     pl.semaphore_wait(barrier, outer + 1)
 
-    spans = (pl.ds(0, part_rows), pl.ds(part_rows, part_rows + SUB))
+    counts = [part_rows] * (PARTS - 1) + [part_rows + SUB]
+    spans = [pl.ds(part * part_rows, count) for part, count in enumerate(counts)]
 
     def ag(part, block, slot, target):
         ref = qg.at[block, spans[part]]
         return send(ref, ref, ag_send.at[part, slot], ag_recv.at[part, block], target)
 
-    for part in range(2):
+    def own_sends(part):
         for step in range(1, outer):
             ag(part, me, step, dev((z + step) % outer, y, c)).start()
         ag(part, me, outer, across).start()
@@ -96,7 +99,7 @@
 
     def widen(part, block):
         first = block * block_rows + part * part_rows
-        count = part_rows + part * SUB
+        count = counts[part]
         qf[pl.ds(pl.multiple_of(first, SUB), count), :] = qg[block, spans[part]].astype(F32)
 
     def from_z(part):
@@ -128,10 +131,13 @@
                 axis=0,
             ).astype(BF16)
 
+    own_sends(0)
     from_z(0)
+    own_sends(1)
     for step in range(outer):
         from_across(0, step)
     from_z(1)
+    own_sends(2)
     loads[5].start()
     from_sibling(0)
     loads[3].wait()
@@ -204,24 +210,28 @@
         return send(sb_z.at[zz], rb_z.at[sender], z_s.at[zz], z_r.at[sender], dev(zz, y, c))
 
     def sibling_slots(zz):
-        slots = [zz * 2 + 1 - y, zz * 2 + y, zz * 2 + 3 - y, zz * 2 + 2 + y]
+        slots = [zz * 2 + 1 - y, zz * 2 + y]
         for slot, found in zip(slots, attend([slot * 2 + 1 - c for slot in slots])):
             write(sb_core.at[slot], found)
             core_copy(slot).start()
 
-    def first_half(i, carry):
-        sibling_slots(2 * i)
-        for step in range(4):
-            from_across(1, 4 * i + step)
-        return carry
-
-    def second_half(i, carry):
-        sibling_slots(outer // 2 + 2 * i)
-        return carry
-
-    lax.fori_loop(0, outer // 4, first_half, 0)
-    from_sibling(1)
-    lax.fori_loop(0, outer // 4, second_half, 0)
+    part_zs = outer // PARTS
+    for part in range(PARTS):
+        if part + 1 < PARTS:
+            for step in range(outer):
+                from_across(part + 1, step)
+        if part + 2 < PARTS:
+            from_z(part + 2)
+        if part + 3 < PARTS:
+            own_sends(part + 3)
+
+        def of_part(i, carry):
+            sibling_slots(part * part_zs + i)
+            return carry
+
+        lax.fori_loop(0, part_zs, of_part, 0)
+        if part + 1 < PARTS:
+            from_sibling(part + 1)
 
     def for_across(i, carry):
         zs = [(z + 1 + 2 * i) % outer, (z + 2 + 2 * i) % outer]
@@ -260,7 +270,7 @@
     def column(first):
         rows = jnp.zeros((n, HD), F32)
         for s in range(CONTROLS):
-            found_rows = qf[pl.ds(2 * part_rows + first + s, n, stride=block_rows), :]
+            found_rows = qf[pl.ds(info_at + first + s, n, stride=block_rows), :]
             rows = jnp.where(section == s, found_rows, rows)
         return jnp.concatenate([rows[:, r:r + 1] for r in range(tokens_dev)], axis=0)
 
@@ -349,10 +359,10 @@
         done[...] = total
         for t in range(SUB):
             out_ref[:, (cc * SUB + t) * HD:(cc * SUB + t + 1) * HD] = (
-                done[pl.ds(t, tokens_dev, stride=SUB), :]
+                done[pl.ds(t, tokens_dev, stride=SUB), :].astype(BF16)
             )
 
-    for part in range(2):
+    for part in range(PARTS):
         for slot in range(1, 4 * outer):
             ag(part, me, slot, across).wait_send()
     for slot in range(2 * outer):
@@ -386,7 +396,7 @@
     dma = pltpu.SemaphoreType.DMA
     return pl.pallas_call(
         functools.partial(kernel, cfg),
-        out_shape=jax.ShapeDtypeStruct((tokens_dev, model), F32),
+        out_shape=jax.ShapeDtypeStruct((tokens_dev, model), BF16),
         in_specs=[pl.BlockSpec(memory_space=pl.ANY)] * 6,
         out_specs=pl.BlockSpec(memory_space=pltpu.VMEM),
         scratch_shapes=[
@@ -415,8 +425,8 @@
             vmem((chunks, outer, tokens_dev * SUB, HD), BF16),
             vmem((tokens_dev * SUB, HD), F32),
             dma((6,)),
-            dma((2, 4 * outer)),
-            dma((2, n)),
+            dma((PARTS, 4 * outer)),
+            dma((PARTS, n)),
             dma((n // 2,)),
             dma((n // 2,)),
             dma((outer,)),
@@ -438,7 +448,7 @@
             bytes_accessed=2 * (2 * keys * width + heads_dev * HD * model),
             transcendentals=tokens * keys * pairs,
         ),
-    )(queries, key_rows, value_rows, out_weight, levels, owner_map).astype(BF16)
+    )(queries, key_rows, value_rows, out_weight, levels, owner_map)
 
 
 def solution(mesh):

time: 44.3 us -> 51.1 us (1.15)
  Pallas kernels: 42.7 us -> 49.6 us
  other arithmetic: 1.47 us -> 0 us
  local copies, waits for them, and re-layouts: 0 us -> 1.39 us
    pallas_call x1, Pallas kernels: 42.7 us -> 49.6 us  [on_device(): pl.pallas_call(functools.partial(kernel, cfg), out_shape=jax.ShapeDtypeSt...]
    convert_element_type x1 -> x0, other arithmetic: 1.47 us -> none  [on_device(): return pl.pallas_call(functools.partial(kernel, cfg), out_shape=jax.Shape...]
    unnamed x0 -> x1, local copies, waits for them, and re-layouts: none -> 1.39 us
where the time goes in v4:
time: 51.1 us; the launch traced here: 51 us
  Pallas kernels  49.6 us (97%)
  local copies, waits for them, and re-layouts  1.39 us (3%)
    pallas_call x1, Pallas kernels, on_device(): pl.pallas_call(functools.partial(kernel, cfg), out_shape=jax.ShapeDtypeSt...  49.6 us
    unnamed x1, local copies, waits for them, and re-layouts  1.39 us

profile of v4, /device:TPU:0, one launch (start us, length us, event | category | flops | bytes accessed | tf_op | source)
XLA Modules:
  0.0 51.0 jit_solution(3521943795833555043)
XLA Ops:
  0.0 49.6 %shard_map.64 = bf16[3,4096]{1,0:T(4,128)(2,1)} custom-call(bf16[3,8192]{1,0:T(4,128)(2,1)} %q_hbm.1, bf16[256,8192]{1,0:T(8,128)(2,1)} %k_hbm.1, bf16[256,8192]{1,0:T(8,128)(2,1)} %v_hbm.1, bf16[512,4096]{1,0:T(8,128)(2,1)} %w_hbm.1, s32[3,3]{1,0:T(4,128)} %level_hbm.1, s32[3,3]{1,0:T(4,128)} %owner_hbm.1), custom_call_target="tpu_custom_call" | custom-call | flops 603979776 | bytes 12582912 | tf_op jit(solution)/shard_map/pallas_call | solution.py:397
  49.6 1.4 %copy.8 = bf16[3,4096]{1,0:T(4,128)(2,1)} copy(bf16[3,4096]{1,0:T(4,128)(2,1)} %shard_map.64) | data formatting | bytes 49152

commit v5 on v2

--- a/solution.py
+++ b/solution.py
@@ -20,18 +20,20 @@
 
 def kernel(
     cfg, q_hbm, k_hbm, v_hbm, w_hbm, level_hbm, owner_hbm, out_ref,
-    k_ref, v_ref, w_ref, q_ref, level_ref, owner_ref, qs, qg, qf, qh,
+    k_ref, v_ref, w_ref, q_ref, level_ref, owner_ref, qs, qg0, qg1, qf, qh,
     sb_core, rb_core, sb_y, rb_y, sb_z, rb_z,
-    pf, pb, rc, sy, ry, sz, rz, done,
+    pf, pb, rc, sp, rp, done,
     load_sem, ag_send, ag_recv,
     core_s, core_r, y_s, y_r, z_s, z_r,
-    pc_s, pc_r, py_s, py_r, pz_s, pz_r,
+    pc_s, pc_r, p_s, p_r,
 ):
     n, outer, tokens_dev, heads_dev, pairs, chunks = cfg
     tokens = tokens_dev * n
     group = lax.axis_index("groups")
     me = lax.axis_index("seq")
-    z, y, c = me // 4, (me // 2) % 2, me % 2
+    z, low = lax.div(me, 4), lax.rem(me, 4)
+    y, c = lax.div(low, 2), lax.rem(low, 2)
+    zs = [lax.rem(z + step, outer) for step in range(1, outer)] + [z]
 
     def dev(zz, yy, cc):
         return (group, zz * 4 + yy * 2 + cc)
@@ -47,16 +49,17 @@
             ]
         )
     ]
-    for load in loads:
+    for load in loads[:5]:
         load.start()
 
     barrier = pltpu.get_barrier_semaphore()
     pl.semaphore_signal(barrier, inc=1, device_id=sibling, device_id_type=MESH)
     pl.semaphore_signal(barrier, inc=1, device_id=across, device_id_type=MESH)
-    for step in range(1, outer):
-        pl.semaphore_signal(
-            barrier, inc=1, device_id=dev((z + step) % outer, y, c), device_id_type=MESH
-        )
+    for zz in zs[:-1]:
+        for yy in (y, 1 - y):
+            pl.semaphore_signal(
+                barrier, inc=1, device_id=dev(zz, yy, c), device_id_type=MESH
+            )
 
     def send(src, dst, s_sem, r_sem, target):
         return pltpu.make_async_remote_copy(
@@ -77,48 +80,62 @@
     qs[2 * part_rows:, :] = jnp.zeros((SUB, HD), F32)
     qs[2 * part_rows:2 * part_rows + CONTROLS, 0:tokens_dev] = owner_ref[...].astype(F32)
     qs[2 * part_rows + 8:2 * part_rows + 8 + CONTROLS, 0:tokens_dev] = level_ref[...].astype(F32)
-    qg[me] = qs[...].astype(BF16)
-    qf[pl.ds(pl.multiple_of(me * block_rows, SUB), block_rows), :] = qs[...]
-
-    pl.semaphore_wait(barrier, outer + 1)
-
-    spans = (pl.ds(0, part_rows), pl.ds(part_rows, part_rows + SUB))
-
-    def ag(part, block, slot, target):
-        ref = qg.at[block, spans[part]]
-        return send(ref, ref, ag_send.at[part, slot], ag_recv.at[part, block], target)
+    place_of = (y * 2 + c) * outer
+    mine_at = place_of + z
+    qg0[mine_at] = qs[0:part_rows, :].astype(BF16)
+    qg1[mine_at] = qs[part_rows:, :].astype(BF16)
+    qf[pl.ds(pl.multiple_of(mine_at * block_rows, SUB), block_rows), :] = qs[...]
+
+    pl.semaphore_wait(barrier, 2 * outer)
+
+    parts = (qg0, qg1)
+    across_at = ((1 - y) * 2 + c) * outer
+
+    def along(part, target_z, sender_z):
+        ref = parts[part].at[mine_at]
+        return send(
+            ref, ref, ag_send.at[part, target_z], ag_recv.at[part, sender_z], dev(target_z, y, c)
+        )
+
+    def cross(part, zz):
+        ref = parts[part].at[place_of + zz]
+        return send(ref, ref, ag_send.at[part, outer + zz], ag_recv.at[part, outer + zz], across)
+
+    def hand(part, second):
+        ref = parts[part].at[pl.ds(across_at if second else place_of, outer)]
+        slot = 2 * outer + second
+        return send(ref, ref, ag_send.at[part, slot], ag_recv.at[part, slot], sibling)
 
     for part in range(2):
-        for step in range(1, outer):
-            ag(part, me, step, dev((z + step) % outer, y, c)).start()
-        ag(part, me, outer, across).start()
-        ag(part, me, 2 * outer, sibling).start()
+        for zz in zs[:-1]:
+            along(part, zz, z).start()
+        cross(part, z).start()
 
     def widen(part, block):
         first = block * block_rows + part * part_rows
         count = part_rows + part * SUB
-        qf[pl.ds(pl.multiple_of(first, SUB), count), :] = qg[block, spans[part]].astype(F32)
+        qf[pl.ds(pl.multiple_of(first, SUB), count), :] = parts[part][block].astype(F32)
 
     def from_z(part):
-        for step in range(1, outer):
-            block = ((z + step) % outer) * 4 + y * 2 + c
-            ag(part, block, step, across).wait_recv()
-            ag(part, block, outer + step, across).start()
-            ag(part, block, 2 * outer + step, sibling).start()
-            widen(part, block)
-
-    def from_across(part, step):
-        block = ((z + step) % outer) * 4 + (1 - y) * 2 + c
-        ag(part, block, step, across).wait_recv()
-        ag(part, block, 3 * outer + step, sibling).start()
-        widen(part, block)
+        for zz in zs[:-1]:
+            along(part, zz, zz).wait_recv()
+            cross(part, zz).start()
+        hand(part, 0).start()
+        for zz in zs[:-1]:
+            widen(part, place_of + zz)
+
+    def from_across(part):
+        for zz in zs[-1:] + zs[:-1]:
+            cross(part, zz).wait_recv()
+        hand(part, 1).start()
+        for zz in zs:
+            widen(part, across_at + zz)
 
     def from_sibling(part):
-        for yy in (y, 1 - y):
-            for step in range(outer):
-                block = ((z + step) % outer) * 4 + yy * 2 + (1 - c)
-                ag(part, block, step, sibling).wait_recv()
-                widen(part, block)
+        for second, yy in ((0, y), (1, 1 - y)):
+            hand(part, second).wait_recv()
+            for zz in range(outer):
+                widen(part, (yy * 2 + 1 - c) * outer + zz)
         for h in range(part_heads):
             qh[part * part_heads + h] = jnp.concatenate(
                 [
@@ -129,9 +146,9 @@
             ).astype(BF16)
 
     from_z(0)
-    for step in range(outer):
-        from_across(0, step)
+    from_across(0)
     from_z(1)
+    loads[5].start()
     from_sibling(0)
     loads[3].wait()
     loads[4].wait()
@@ -200,25 +217,21 @@
             write(sb_core.at[slot], found)
             core_copy(slot).start()
 
-    def first_half(i, carry):
+    def sibling_step(i, carry):
         sibling_slots(i)
-        from_across(1, 2 * i)
-        from_across(1, 2 * i + 1)
         return carry
 
-    def second_half(i, carry):
-        sibling_slots(outer // 2 + i)
-        return carry
-
-    lax.fori_loop(0, outer // 2, first_half, 0)
+    lax.fori_loop(0, outer // 4, sibling_step, 0)
+    from_across(1)
+    lax.fori_loop(outer // 4, outer // 2, sibling_step, 0)
     from_sibling(1)
-    lax.fori_loop(0, outer // 2, second_half, 0)
+    lax.fori_loop(outer // 2, outer, sibling_step, 0)
 
     def for_across(i, carry):
-        zs = [(z + 1 + 2 * i) % outer, (z + 2 + 2 * i) % outer]
-        slots = [zz * 2 + 1 - y for zz in zs]
+        pair = [lax.rem(z + 1 + 2 * i, outer), lax.rem(z + 2 + 2 * i, outer)]
+        slots = [zz * 2 + 1 - y for zz in pair]
         both = attend([slot * 2 + c for slot in slots])
-        for zz, slot, found in zip(zs, slots, both):
+        for zz, slot, found in zip(pair, slots, both):
             core_copy(slot).wait_recv()
             write(sb_y.at[zz], merge(found, [rb_core.at[slot]]))
             y_copy(zz).start()
@@ -233,20 +246,20 @@
         return merge(found, [rb_core.at[slot], rb_y.at[zz]])
 
     def for_z(i, carry):
-        zs = [(z + 1 + 2 * i) % outer, (z + 2 + 2 * i) % outer]
-        for zz, found in zip(zs, attend([zz * 4 + y * 2 + c for zz in zs])):
+        pair = [lax.rem(z + 1 + 2 * i, outer), lax.rem(z + 2 + 2 * i, outer)]
+        for zz, found in zip(pair, attend([zz * 4 + y * 2 + c for zz in pair])):
             write(sb_z.at[zz], collect(zz, found))
             z_copy(zz, z).start()
         return carry
 
     lax.fori_loop(0, outer // 2 - 1, for_z, 0)
-    final = (z + outer - 1) % outer
+    final = zs[-2]
     found, mine = attend([final * 4 + y * 2 + c, me])
     write(sb_z.at[final], collect(final, found))
     z_copy(final, z).start()
     mine = collect(z, mine)
 
-    section = me * heads_dev // HEADS
+    section = lax.div(me * heads_dev, HEADS)
 
     def column(first):
         rows = jnp.zeros((n, HD), F32)
@@ -255,8 +268,10 @@
             rows = jnp.where(section == s, found_rows, rows)
         return jnp.concatenate([rows[:, r:r + 1] for r in range(tokens_dev)], axis=0)
 
-    position = lax.broadcasted_iota(jnp.int32, (n, 1), 0) * tokens_dev
-    position = jnp.concatenate([position + r for r in range(tokens_dev)], axis=0).astype(F32)
+    block = lax.broadcasted_iota(jnp.int32, (n, 1), 0).astype(F32)
+    line = jnp.floor((block + 0.5) * (1.0 / outer))
+    position = ((block - line * outer) * 4 + line) * tokens_dev
+    position = jnp.concatenate([position + r for r in range(tokens_dev)], axis=0)
     is_base = section >= CONTROLS
     owner = jnp.where(is_base, position, column(0))
     level = jnp.where(is_base, float(LEVELS), column(8))
@@ -270,16 +285,16 @@
     level = jnp.broadcast_to(level, (tokens, HD)).astype(BF16)
     row_weight = jnp.dot(picked, level, preferred_element_type=F32)[:, 0:1] / LEVELS
 
-    for step in range(1, outer):
-        z_copy((z + step) % outer, (z + step) % outer).wait_recv()
-    sums, stat = merge(mine, [rb_z.at[(z + step) % outer] for step in range(1, outer)])
+    for zz in zs[:-1]:
+        z_copy(zz, zz).wait_recv()
+    sums, stat = merge(mine, [rb_z.at[zz] for zz in zs[:-1]])
     attended = jnp.concatenate(
         [(sums[j] / stat[:, mid + j:mid + j + 1]).astype(BF16) for j in range(heads_dev)], axis=1
     )
     chosen = jnp.dot(picked, attended, preferred_element_type=F32).astype(BF16)
 
     loads[5].wait()
-    half, quarter, piece = tokens // 2 * SUB, tokens // 4 * SUB, tokens_dev * SUB
+    half, piece = tokens // 2 * SUB, tokens_dev * SUB
 
     def rows_at(first, count):
         return pl.ds(pl.multiple_of(first, SUB), count)
@@ -288,12 +303,10 @@
         rows = rows_at((1 - c) * half, half)
         return send(pb.at[cc, rows], rc.at[cc], pc_s.at[cc], pc_r.at[cc], sibling)
 
-    def py_copy(cc):
-        return send(sy.at[cc], ry.at[cc], py_s.at[cc], py_r.at[cc], across)
-
-    def pz_copy(cc, zz, sender):
+    def p_copy(zz, yy, sender_z, sender_y):
         return send(
-            sz.at[cc, zz], rz.at[cc, sender], pz_s.at[cc, zz], pz_r.at[cc, sender], dev(zz, y, c)
+            sp.at[yy * outer + zz], rp.at[sender_y * outer + sender_z],
+            p_s.at[yy * outer + zz], p_r.at[sender_y * outer + sender_z], dev(zz, yy, c),
         )
 
     width = 4 * HD
@@ -313,30 +326,23 @@
 
     for cc in range(chunks):
         pc_copy(cc).wait_recv()
-        away, near = rows_at((1 - y) * quarter, quarter), rows_at(y * quarter, quarter)
-        away_own = rows_at(c * half + (1 - y) * quarter, quarter)
-        sy[cc] = (pf[cc, away_own] + rc[cc, away].astype(F32)).astype(BF16)
-        py_copy(cc).start()
+
+    def partial_sum(cc, zz, yy):
+        at = (yy * outer + zz) * piece
+        return pf[cc, rows_at(c * half + at, piece)] + rc[cc, rows_at(at, piece)].astype(F32)
+
+    peers = [(zz, yy) for zz in zs[:-1] for yy in (1 - y, y)] + [(z, 1 - y)]
+    for zz, yy in peers:
+        for cc in range(chunks):
+            sp[yy * outer + zz, cc] = partial_sum(cc, zz, yy).astype(BF16)
+        p_copy(zz, yy, z, y).start()
+    totals = [partial_sum(cc, z, y) for cc in range(chunks)]
+    for zz, yy in peers:
+        p_copy(zz, yy, zz, yy).wait_recv()
     for cc in range(chunks):
-        py_copy(cc).wait_recv()
-        for step in range(1, outer):
-            zz = (z + step) % outer
-            own = rows_at(c * half + y * quarter + zz * piece, piece)
-            from_core = rows_at(y * quarter + zz * piece, piece)
-            from_y = rows_at(zz * piece, piece)
-            sz[cc, zz] = (
-                pf[cc, own] + rc[cc, from_core].astype(F32) + ry[cc, from_y].astype(F32)
-            ).astype(BF16)
-            pz_copy(cc, zz, z).start()
-    for cc in range(chunks):
-        own = rows_at(c * half + y * quarter + z * piece, piece)
-        from_core = rows_at(y * quarter + z * piece, piece)
-        from_y = rows_at(z * piece, piece)
-        total = pf[cc, own] + rc[cc, from_core].astype(F32) + ry[cc, from_y].astype(F32)
-        for step in range(1, outer):
-            sender = (z + step) % outer
-            pz_copy(cc, sender, sender).wait_recv()
-            total = total + rz[cc, sender].astype(F32)
+        total = totals[cc]
+        for zz, yy in peers:
+            total = total + rp[yy * outer + zz, cc].astype(F32)
         done[...] = total
         for t in range(SUB):
             out_ref[:, (cc * SUB + t) * HD:(cc * SUB + t + 1) * HD] = (
@@ -344,19 +350,22 @@
             )
 
     for part in range(2):
-        for slot in range(1, 4 * outer):
-            ag(part, me, slot, across).wait_send()
+        for zz in zs[:-1]:
+            along(part, zz, z).wait_send()
+        for zz in range(outer):
+            cross(part, zz).wait_send()
+        hand(part, 0).wait_send()
+        hand(part, 1).wait_send()
     for slot in range(2 * outer):
         core_copy(slot).wait_send()
     for zz in range(outer):
         y_copy(zz).wait_send()
-    for step in range(1, outer):
-        z_copy((z + step) % outer, z).wait_send()
+    for zz in zs[:-1]:
+        z_copy(zz, z).wait_send()
     for cc in range(chunks):
         pc_copy(cc).wait_send()
-        py_copy(cc).wait_send()
-        for step in range(1, outer):
-            pz_copy(cc, (z + step) % outer, z).wait_send()
+    for zz, yy in peers:
+        p_copy(zz, yy, z, y).wait_send()
 
 
 def on_device(queries, key_rows, value_rows, out_weight, levels, owner_map):
@@ -388,7 +397,8 @@
             vmem(levels.shape, jnp.int32),
             vmem(owner_map.shape, jnp.int32),
             vmem((block_rows, HD), F32),
-            vmem((n, block_rows, HD), BF16),
+            vmem((n, block_rows // 2 - SUB // 2, HD), BF16),
+            vmem((n, block_rows // 2 + SUB // 2, HD), BF16),
             vmem((n * block_rows, HD), F32),
             vmem((pairs, tokens, HD), BF16),
             vmem((n // 2,) + message, BF16),
@@ -400,14 +410,12 @@
             vmem((chunks, tokens * SUB, HD), F32),
             vmem((chunks, tokens * SUB, HD), BF16),
             vmem((chunks, tokens // 2 * SUB, HD), BF16),
-            vmem((chunks, tokens // 4 * SUB, HD), BF16),
-            vmem((chunks, tokens // 4 * SUB, HD), BF16),
-            vmem((chunks, outer, tokens_dev * SUB, HD), BF16),
-            vmem((chunks, outer, tokens_dev * SUB, HD), BF16),
+            vmem((2 * outer, chunks, tokens_dev * SUB, HD), BF16),
+            vmem((2 * outer, chunks, tokens_dev * SUB, HD), BF16),
             vmem((tokens_dev * SUB, HD), F32),
             dma((6,)),
-            dma((2, 4 * outer)),
-            dma((2, n)),
+            dma((2, 2 * outer + 2)),
+            dma((2, 2 * outer + 2)),
             dma((n // 2,)),
             dma((n // 2,)),
             dma((outer,)),
@@ -416,10 +424,8 @@
             dma((outer,)),
             dma((chunks,)),
             dma((chunks,)),
-            dma((chunks,)),
-            dma((chunks,)),
-            dma((chunks, outer)),
-            dma((chunks, outer)),
+            dma((2 * outer,)),
+            dma((2 * outer,)),
         ],
         compiler_params=pltpu.CompilerParams(
             collective_id=0, has_side_effects=True, vmem_limit_bytes=56 * 1024 * 1024

time: 44.2 us -> 42.4 us (0.959)
  Pallas kernels: 42.6 us -> 40.8 us
    pallas_call x1, Pallas kernels: 42.6 us -> 40.8 us  [on_device(): pl.pallas_call(functools.partial(kernel, cfg), out_shape=jax.ShapeDtypeSt...]
where the time goes in v5:
time: 42.4 us; the launch traced here: 42.2 us
  Pallas kernels  40.8 us (96%)
  local copies, waits for them, and re-layouts  1.39 us (3%)
    pallas_call x1, Pallas kernels, on_device(): pl.pallas_call(functools.partial(kernel, cfg), out_shape=jax.ShapeDtypeSt...  40.8 us
    unnamed x1, local copies, waits for them, and re-layouts  1.39 us

profile of v5, /device:TPU:0, one launch (start us, length us, event | category | flops | bytes accessed | tf_op | source)
XLA Modules:
  0.0 42.2 jit_solution(3759657108644362911)
XLA Ops:
  0.0 40.8 %shard_map.64 = bf16[3,4096]{1,0:T(4,128)(2,1)} custom-call(bf16[3,8192]{1,0:T(4,128)(2,1)} %q_hbm.1, bf16[256,8192]{1,0:T(8,128)(2,1)} %k_hbm.1, bf16[256,8192]{1,0:T(8,128)(2,1)} %v_hbm.1, bf16[512,4096]{1,0:T(8,128)(2,1)} %w_hbm.1, s32[3,3]{1,0:T(4,128)} %level_hbm.1, s32[3,3]{1,0:T(4,128)} %owner_hbm.1), custom_call_target="tpu_custom_call" | custom-call | flops 603979776 | bytes 12582912 | tf_op jit(solution)/shard_map/pallas_call | solution.py:387
  40.8 1.4 %copy.8 = bf16[3,4096]{1,0:T(4,128)(2,1)} copy(bf16[3,4096]{1,0:T(4,128)(2,1)} %shard_map.64) | data formatting | bytes 49152

commit v6 on v5

--- a/solution.py
+++ b/solution.py
@@ -211,33 +211,43 @@
     def z_copy(zz, sender):
         return send(sb_z.at[zz], rb_z.at[sender], z_s.at[zz], z_r.at[sender], dev(zz, y, c))
 
-    def sibling_slots(zz):
-        slots = [zz * 2 + 1 - y, zz * 2 + y]
+    def for_sibling(pair, yy):
+        slots = [zz * 2 + yy for zz in pair]
         for slot, found in zip(slots, attend([slot * 2 + 1 - c for slot in slots])):
             write(sb_core.at[slot], found)
             core_copy(slot).start()
 
-    def sibling_step(i, carry):
-        sibling_slots(i)
-        return carry
-
-    lax.fori_loop(0, outer // 4, sibling_step, 0)
-    from_across(1)
-    lax.fori_loop(outer // 4, outer // 2, sibling_step, 0)
-    from_sibling(1)
-    lax.fori_loop(outer // 2, outer, sibling_step, 0)
-
-    def for_across(i, carry):
-        pair = [lax.rem(z + 1 + 2 * i, outer), lax.rem(z + 2 + 2 * i, outer)]
+    def for_across(pair):
         slots = [zz * 2 + 1 - y for zz in pair]
         both = attend([slot * 2 + c for slot in slots])
         for zz, slot, found in zip(pair, slots, both):
             core_copy(slot).wait_recv()
             write(sb_y.at[zz], merge(found, [rb_core.at[slot]]))
             y_copy(zz).start()
+
+    def ring_pair(i):
+        return [lax.rem(z + 1 + 2 * i, outer), lax.rem(z + 2 + 2 * i, outer)]
+
+    def pairs_of(part, step):
+        def body(i, carry):
+            first = part * (outer // 2) + 2 * i
+            step([first, first + 1])
+            return carry
+
+        lax.fori_loop(0, outer // 4, body, 0)
+
+    pairs_of(0, lambda pair: for_sibling(pair, 1 - y))
+    from_across(1)
+    pairs_of(0, for_across)
+    from_sibling(1)
+    pairs_of(1, lambda pair: for_sibling(pair, 1 - y))
+    pairs_of(1, for_across)
+
+    def own_line(i, carry):
+        for_sibling(ring_pair(i), y)
         return carry
 
-    lax.fori_loop(0, outer // 2, for_across, 0)
+    lax.fori_loop(0, outer // 2, own_line, 0)
 
     def collect(zz, found):
         slot = zz * 2 + y
@@ -246,7 +256,7 @@
         return merge(found, [rb_core.at[slot], rb_y.at[zz]])
 
     def for_z(i, carry):
-        pair = [lax.rem(z + 1 + 2 * i, outer), lax.rem(z + 2 + 2 * i, outer)]
+        pair = ring_pair(i)
         for zz, found in zip(pair, attend([zz * 4 + y * 2 + c for zz in pair])):
             write(sb_z.at[zz], collect(zz, found))
             z_copy(zz, z).start()

time: 42.4 us -> 40.8 us (0.962)
  Pallas kernels: 40.8 us -> 39.2 us
    pallas_call x1, Pallas kernels: 40.8 us -> 39.2 us  [on_device(): pl.pallas_call(functools.partial(kernel, cfg), out_shape=jax.ShapeDtypeSt...]
where the time goes in v6:
time: 40.8 us; the launch traced here: 40.6 us
  Pallas kernels  39.2 us (96%)
  local copies, waits for them, and re-layouts  1.39 us (3%)
    pallas_call x1, Pallas kernels, on_device(): pl.pallas_call(functools.partial(kernel, cfg), out_shape=jax.ShapeDtypeSt...  39.2 us
    unnamed x1, local copies, waits for them, and re-layouts  1.39 us

profile of v6, /device:TPU:0, one launch (start us, length us, event | category | flops | bytes accessed | tf_op | source)
XLA Modules:
  0.0 40.6 jit_solution(10015506312326214151)
XLA Ops:
  0.0 39.2 %shard_map.64 = bf16[3,4096]{1,0:T(4,128)(2,1)} custom-call(bf16[3,8192]{1,0:T(4,128)(2,1)} %q_hbm.1, bf16[256,8192]{1,0:T(8,128)(2,1)} %k_hbm.1, bf16[256,8192]{1,0:T(8,128)(2,1)} %v_hbm.1, bf16[512,4096]{1,0:T(8,128)(2,1)} %w_hbm.1, s32[3,3]{1,0:T(4,128)} %level_hbm.1, s32[3,3]{1,0:T(4,128)} %owner_hbm.1), custom_call_target="tpu_custom_call" | custom-call | flops 603979776 | bytes 12582912 | tf_op jit(solution)/shard_map/pallas_call | solution.py:397
  39.2 1.4 %copy.8 = bf16[3,4096]{1,0:T(4,128)(2,1)} copy(bf16[3,4096]{1,0:T(4,128)(2,1)} %shard_map.64) | data formatting | bytes 49152

commit v7 on v6

--- a/solution.py
+++ b/solution.py
@@ -49,7 +49,7 @@
             ]
         )
     ]
-    for load in loads[:5]:
+    for load in loads[:3]:
         load.start()
 
     barrier = pltpu.get_barrier_semaphore()
@@ -110,6 +110,8 @@
         for zz in zs[:-1]:
             along(part, zz, z).start()
         cross(part, z).start()
+    loads[3].start()
+    loads[4].start()
 
     def widen(part, block):
         first = block * block_rows + part * part_rows

time: 40.8 us -> 40.8 us (level)
  no operation moved by 1% of the time
where the time goes in v7:
time: 40.8 us; the launch traced here: 40.6 us
  Pallas kernels  39.2 us (96%)
  local copies, waits for them, and re-layouts  1.39 us (3%)
    pallas_call x1, Pallas kernels, on_device(): pl.pallas_call(functools.partial(kernel, cfg), out_shape=jax.ShapeDtypeSt...  39.2 us
    unnamed x1, local copies, waits for them, and re-layouts  1.39 us

profile of v7, /device:TPU:0, one launch (start us, length us, event | category | flops | bytes accessed | tf_op | source)
XLA Modules:
  0.0 40.6 jit_solution(6329636459110926222)
XLA Ops:
  0.0 39.2 %shard_map.64 = bf16[3,4096]{1,0:T(4,128)(2,1)} custom-call(bf16[3,8192]{1,0:T(4,128)(2,1)} %q_hbm.1, bf16[256,8192]{1,0:T(8,128)(2,1)} %k_hbm.1, bf16[256,8192]{1,0:T(8,128)(2,1)} %v_hbm.1, bf16[512,4096]{1,0:T(8,128)(2,1)} %w_hbm.1, s32[3,3]{1,0:T(4,128)} %level_hbm.1, s32[3,3]{1,0:T(4,128)} %owner_hbm.1), custom_call_target="tpu_custom_call" | custom-call | flops 603979776 | bytes 12582912 | tf_op jit(solution)/shard_map/pallas_call | solution.py:399
  39.2 1.4 %copy.8 = bf16[3,4096]{1,0:T(4,128)(2,1)} copy(bf16[3,4096]{1,0:T(4,128)(2,1)} %shard_map.64) | data formatting | bytes 49152
